TPU v7x, 128 devices: a whole 4x4x4 slice. The times are simulated.
128 devices in a mesh: section: 2 (over x_hi), dp: 32 (over z, y, core), tensor: 2 (over x_lo).
Axes of the slice: x: 4 (x_hi: 2, x_lo: 2; x = x_hi * 2 + x_lo), y: 4, z: 4, core: 2. Of those that a mesh axis runs over, the one named last changes fastest.
Arguments:
- layer_input: bfloat16 [64, 128, 1024], P('dp', 'tensor'), may hold values from -6 to 6
- lengths: int32 [64, 4], P('dp'), may hold values from 1 to 96, 128 in all within a row
- cotangent: bfloat16 [64, 128, 1024], P('dp', 'tensor'), may hold values from -6 to 6
- norm1_gain: bfloat16 [2, 1024], P('section'), may hold values from 0.5 to 1.5
- norm1_shift: bfloat16 [2, 1024], P('section'), may hold values from -1.5 to 1.5
- qkv_weight: bfloat16 [2, 1024, 3, 1024], P('section', 'dp', None, 'tensor'), may hold values from -0.1875 to 0.1875
- qkv_bias: bfloat16 [2, 3, 1024], P('section', None, 'tensor'), may hold values from -1 to 1
- dense_weight: bfloat16 [2, 1024, 1024], P('section', 'dp', 'tensor'), may hold values from -0.5 to 0.5
- dense_bias: bfloat16 [2, 1024], P('section'), may hold values from -1 to 1
- norm2_gain: bfloat16 [2, 1024], P('section'), may hold values from 0.5 to 1.5
- norm2_shift: bfloat16 [2, 1024], P('section'), may hold values from -1.5 to 1.5
- up_weight: bfloat16 [2, 1024, 4096], P('section', 'dp', 'tensor'), may hold values from -0.1875 to 0.1875
- up_bias: bfloat16 [2, 4096], P('section', 'tensor'), may hold values from -1 to 1
- down_weight: bfloat16 [2, 1024, 4096], P('section', 'dp', 'tensor'), may hold values from -0.09375 to 0.09375
- down_bias: bfloat16 [2, 1024], P('section'), may hold values from -1 to 1
Outputs:
- layer_out: bfloat16 [2, 64, 128, 1024], P('section', 'dp', 'tensor')
- input_grad: bfloat16 [2, 64, 128, 1024], P('section', 'dp', 'tensor')
- grad_norm1_gain: float32 [2, 1024], P('section')
- grad_norm1_shift: float32 [2, 1024], P('section')
- grad_qkv_weight: float32 [2, 1024, 3, 1024], P('section', 'dp', None, 'tensor')
- grad_qkv_bias: float32 [2, 3, 1024], P('section', None, 'tensor')
- grad_dense_weight: float32 [2, 1024, 1024], P('section', 'dp', 'tensor')
- grad_dense_bias: float32 [2, 1024], P('section')
- grad_norm2_gain: float32 [2, 1024], P('section')
- grad_norm2_shift: float32 [2, 1024], P('section')
- grad_up_weight: float32 [2, 1024, 4096], P('section', 'dp', 'tensor')
- grad_up_bias: float32 [2, 4096], P('section', 'tensor')
- grad_down_weight: float32 [2, 1024, 4096], P('section', 'dp', 'tensor')
- grad_down_bias: float32 [2, 1024], P('section')
Inputs may be any that keep to these rules, and one draw needn't show every extreme that they name: Each sequence's 4 lengths add up to 128; the longest is exactly 96.
All inputs are finite; a program needn't handle non-finite values.
Results may differ from a plain program's by a relative error of at most 0.025.
Values may be sent and summed in bfloat16 or wider, within the bound.
A program may use at most 128 MiB of HBM per device.

v0:
```python
import jax
import jax.numpy as jnp
from jax import lax
from jax.sharding import PartitionSpec as P

D = 1024
HEADS = 16
HEAD_DIM = 64
FF = 4096
ROWS = 128
MICRO = 2


EPSILON = 1e-05


def shifted(block, axis, distance):
    devices = range(lax.axis_size(axis))
    route = [(i - distance, i) for i in devices if i - distance in devices]
    return lax.ppermute(block, axis, route)


def layer_norm(values, gain, shift):
    centred = values - jnp.mean(values, axis=-1, keepdims=True)
    inverse = lax.rsqrt(jnp.mean(centred * centred, axis=-1, keepdims=True) + EPSILON)
    return centred * inverse * gain + shift


def smooth_gate(values):
    return jax.nn.gelu(values, approximate=True)


def segment_ids(lengths, row_count):
    ends = jnp.cumsum(lengths, axis=-1)
    places = jnp.arange(row_count, dtype=jnp.int32)
    return jnp.sum((places[:, None] >= ends[..., None, :]).astype(jnp.int32), axis=-1)


def contract_rows(left, right):
    return lax.dot_general(
        left, right, (((0,), (0,)), ((), ())), preferred_element_type=jnp.float32
    )


def contract_last(left, right):
    return lax.dot_general(
        left, right, (((1,), (1,)), ((), ())), preferred_element_type=jnp.float32
    )


def keep_where(stacked, position, usable, value):
    current = lax.dynamic_index_in_dim(stacked, position, 0, keepdims=False)
    return lax.dynamic_update_index_in_dim(stacked, jnp.where(usable, value, current), position, 0)


def score_block(queries, keys, offset, segments, slopes):
    block_rows = queries.shape[0]
    key_places = jnp.arange(keys.shape[0], dtype=jnp.int32)
    query_places = offset + jnp.arange(block_rows, dtype=jnp.int32)
    distance = (query_places[:, None] - key_places[None, :]).astype(jnp.float32)
    allowed = (segments[:, None] == segments[None, :]) & (
        key_places[None, :] <= query_places[:, None]
    )
    scores = (
        jnp.einsum("qhd,khd->hqk", queries, keys, preferred_element_type=jnp.float32)
        * HEAD_DIM ** (-0.5)
        - slopes[:, None, None] * distance[None]
    )
    return jnp.where(allowed[None], scores, -1e30)


def attend_forward(queries, keys, values, segments, slopes):
    row_count, heads, depth = queries.shape
    block_rows = min(row_count, 512)
    offsets = jnp.arange(row_count // block_rows, dtype=jnp.int32) * block_rows

    def one_block(offset):
        scores = score_block(queries, keys, offset, segments, slopes)
        highest = jnp.max(scores, axis=-1, keepdims=True)
        exponent = jnp.exp(scores - highest)
        totals = jnp.sum(exponent, axis=-1, keepdims=True)
        chances = (exponent / totals).astype(jnp.bfloat16)
        mixed = jnp.einsum("hqk,khd->qhd", chances, values, preferred_element_type=jnp.float32)
        return (mixed.astype(jnp.bfloat16), (highest + jnp.log(totals))[:, :, 0])

    mixed, log_totals = lax.map(one_block, offsets)
    return (
        mixed.reshape(row_count, heads * depth),
        jnp.transpose(log_totals, (1, 0, 2)).reshape(heads, row_count),
    )


def attend_backward(queries, keys, values, segments, slopes, log_totals, out_grad):
    row_count, heads, depth = queries.shape
    block_rows = min(row_count, 512)
    offsets = jnp.arange(row_count // block_rows, dtype=jnp.int32) * block_rows

    def one_block(totals, offset):
        key_grad, value_grad = totals
        scores = score_block(queries, keys, offset, segments, slopes)
        chances = jnp.exp(scores - log_totals[:, :, None])
        chance_grad = jnp.einsum(
            "qhd,khd->hqk", out_grad, values, preferred_element_type=jnp.float32
        )
        value_grad = value_grad + jnp.einsum(
            "hqk,qhd->khd",
            chances.astype(jnp.bfloat16),
            out_grad,
            preferred_element_type=jnp.float32,
        )
        inner_sum = jnp.sum(chances * chance_grad, axis=-1, keepdims=True)
        score_grad = (chances * (chance_grad - inner_sum)).astype(jnp.bfloat16)
        query_grad = jnp.einsum(
            "hqk,khd->qhd", score_grad, keys, preferred_element_type=jnp.float32
        ) * HEAD_DIM ** (-0.5)
        key_grad = key_grad + jnp.einsum(
            "hqk,qhd->khd", score_grad, queries, preferred_element_type=jnp.float32
        ) * HEAD_DIM ** (-0.5)
        return ((key_grad, value_grad), query_grad)

    zeros = jnp.zeros((row_count, heads, depth), jnp.float32)
    (key_grad, value_grad), query_grad = lax.scan(one_block, (zeros, zeros), offsets)
    return (query_grad.reshape(row_count, heads, depth), key_grad, value_grad)


def forward_tick(current, segments, slopes, weights, small):
    w_qkv, w_dense, w_up, w_down = weights
    gain_one, shift_one, qkv_bias, dense_bias, gain_two, shift_two, up_bias, down_bias = small
    normed = layer_norm(current, gain_one, shift_one).astype(jnp.bfloat16)
    normed_all = lax.all_gather(normed, "tensor", axis=0, tiled=True)
    row_count = normed_all.shape[0]
    flat_qkv = w_qkv.reshape(w_qkv.shape[0], -1)
    projected = (
        jnp.dot(normed_all, flat_qkv, preferred_element_type=jnp.float32).reshape(row_count, 3, -1)
        + qkv_bias
    ).astype(jnp.bfloat16)
    heads_here = projected.shape[2] // HEAD_DIM
    split_heads = projected.reshape(row_count, 3, heads_here, HEAD_DIM)
    mixed, log_totals = attend_forward(
        split_heads[:, 0], split_heads[:, 1], split_heads[:, 2], segments, slopes
    )
    attended = lax.psum_scatter(
        contract_last(mixed, w_dense).astype(jnp.bfloat16),
        "tensor",
        scatter_dimension=0,
        tiled=True,
    ).astype(jnp.float32)
    hidden = current + dense_bias + attended
    normed_two = layer_norm(hidden, gain_two, shift_two).astype(jnp.bfloat16)
    normed_two_all = lax.all_gather(normed_two, "tensor", axis=0, tiled=True)
    raised = jnp.dot(normed_two_all, w_up, preferred_element_type=jnp.float32) + up_bias
    activated = smooth_gate(raised).astype(jnp.bfloat16)
    lowered = lax.psum_scatter(
        contract_last(activated, w_down).astype(jnp.bfloat16),
        "tensor",
        scatter_dimension=0,
        tiled=True,
    ).astype(jnp.float32)
    result = hidden + down_bias + lowered
    return (
        result,
        (current, normed_all, projected, mixed, log_totals, hidden, normed_two_all, raised),
    )


def backward_tick(out_grad, stored, segments, slopes, weights, small, sums, flag):
    w_qkv, w_dense, w_up, w_down = weights
    gain_one, shift_one, qkv_bias, dense_bias, gain_two, shift_two, up_bias, down_bias = small
    current, normed_all, projected, mixed, log_totals, hidden, normed_two_all, raised = stored
    row_count = normed_all.shape[0]
    flag_low = flag.astype(jnp.bfloat16)
    activated = smooth_gate(raised).astype(jnp.bfloat16)
    portion = lax.all_gather(out_grad.astype(jnp.bfloat16), "tensor", axis=0, tiled=True)
    down_grad = sums[3]
    gate_grad = jnp.dot(portion, w_down, preferred_element_type=jnp.float32)
    down_grad = down_grad + contract_rows(portion * flag_low, activated)
    gate_grad, down_part = (gate_grad, down_grad)
    unused_value, gate_pull = jax.vjp(smooth_gate, raised)
    raised_grad = gate_pull(gate_grad)[0].astype(jnp.bfloat16)
    up_bias_grad = jnp.sum(raised_grad.astype(jnp.float32), axis=0)
    normed_two_grad = lax.psum_scatter(
        contract_last(raised_grad, w_up).astype(jnp.bfloat16),
        "tensor",
        scatter_dimension=0,
        tiled=True,
    ).astype(jnp.float32)
    unused_norm, norm_two_pull = jax.vjp(layer_norm, hidden, gain_two, shift_two)
    hidden_part, gain_two_grad, shift_two_grad = norm_two_pull(normed_two_grad)
    hidden_grad = out_grad + hidden_part
    portion = lax.all_gather(hidden_grad.astype(jnp.bfloat16), "tensor", axis=0, tiled=True)
    dense_grad = sums[1]
    mixed_grad = jnp.dot(portion, w_dense, preferred_element_type=jnp.float32)
    dense_grad = dense_grad + contract_rows(portion * flag_low, mixed)
    mixed_grad, dense_part = (mixed_grad, dense_grad)
    heads_here = projected.shape[2] // HEAD_DIM
    split_heads = projected.reshape(row_count, 3, heads_here, HEAD_DIM)
    query_grad, key_grad, value_grad = attend_backward(
        split_heads[:, 0],
        split_heads[:, 1],
        split_heads[:, 2],
        segments,
        slopes,
        log_totals,
        mixed_grad.astype(jnp.bfloat16).reshape(row_count, heads_here, HEAD_DIM),
    )
    projected_grad = (
        jnp.stack([query_grad, key_grad, value_grad], axis=1)
        .reshape(row_count, -1)
        .astype(jnp.bfloat16)
    )
    qkv_bias_grad = jnp.sum(projected_grad.astype(jnp.float32), axis=0).reshape(3, -1)
    flat_qkv = w_qkv.reshape(w_qkv.shape[0], -1)
    normed_grad = lax.psum_scatter(
        contract_last(projected_grad, flat_qkv).astype(jnp.bfloat16),
        "tensor",
        scatter_dimension=0,
        tiled=True,
    ).astype(jnp.float32)
    unused_first, norm_one_pull = jax.vjp(layer_norm, current, gain_one, shift_one)
    current_part, gain_one_grad, shift_one_grad = norm_one_pull(normed_grad)
    input_grad = hidden_grad + current_part
    dense_bias_grad = jnp.sum(hidden_grad, axis=0)
    down_bias_grad = jnp.sum(out_grad, axis=0)
    qkv_grad = sums[0] + contract_rows(normed_all, projected_grad * flag_low).reshape(w_qkv.shape)
    up_grad = sums[2] + contract_rows(normed_two_all, raised_grad * flag_low)
    grad_part = (qkv_grad, dense_part, up_grad, down_part)
    small_grads = (
        gain_one_grad,
        shift_one_grad,
        qkv_bias_grad,
        dense_bias_grad,
        gain_two_grad,
        shift_two_grad,
        up_bias_grad,
        down_bias_grad,
    )
    return (input_grad, grad_part, small_grads)


def local(
    layer_input,
    lengths,
    cotangent,
    norm1_gain,
    norm1_shift,
    qkv_weight,
    qkv_bias,
    dense_weight,
    dense_bias,
    norm2_gain,
    norm2_shift,
    up_weight,
    up_bias,
    down_weight,
    down_bias,
):
    section_index = lax.axis_index("section")
    tensor_index = lax.axis_index("tensor")
    heads_here = qkv_weight.shape[3] // HEAD_DIM
    head_ids = tensor_index * heads_here + jnp.arange(heads_here, dtype=jnp.int32)
    slopes = jnp.exp2(-8.0 * (head_ids + 1).astype(jnp.float32) / HEADS)
    shards = (qkv_weight[0], dense_weight[0], up_weight[0], down_weight[0])
    weights = (
        lax.all_gather(shards[0], "dp", axis=0, tiled=True),
        lax.all_gather(shards[1], "dp", axis=0, tiled=True),
        lax.all_gather(shards[2], "dp", axis=0, tiled=True),
        lax.all_gather(shards[3], "dp", axis=0, tiled=True),
    )
    small = tuple(
        (
            member[0].astype(jnp.float32)
            for member in (
                norm1_gain,
                norm1_shift,
                qkv_bias,
                dense_bias,
                norm2_gain,
                norm2_shift,
                up_bias,
                down_bias,
            )
        )
    )
    inputs = layer_input.astype(jnp.float32)
    local_rows = inputs.shape[1]
    incoming = jnp.zeros((local_rows, inputs.shape[2]), jnp.bfloat16)
    outputs = jnp.zeros(layer_input.shape, jnp.bfloat16)
    stored_all = None
    for tick_index in range(MICRO + 1):
        micro_step = tick_index - section_index
        usable = (micro_step >= 0) & (micro_step < MICRO)
        position = jnp.clip(micro_step, 0, MICRO - 1)
        current = jnp.where(
            section_index == 0, inputs[min(tick_index, MICRO - 1)], incoming.astype(jnp.float32)
        )
        segments = segment_ids(lax.dynamic_index_in_dim(lengths, position, 0, keepdims=False), ROWS)
        result, stored = forward_tick(current, segments, slopes, weights, small)
        if stored_all is None:
            stored_all = tuple(
                (jnp.zeros((MICRO,) + member.shape, member.dtype) for member in stored)
            )
        stored_all = tuple(
            (
                keep_where(stack, position, usable, member)
                for stack, member in zip(stored_all, stored)
            )
        )
        sent = result.astype(jnp.bfloat16)
        outputs = keep_where(outputs, position, usable, sent)
        if tick_index < MICRO:
            incoming = shifted(sent, "section", 1)
    out_grads = cotangent.astype(jnp.float32)
    incoming_grad = jnp.zeros((local_rows, inputs.shape[2]), jnp.bfloat16)
    in_grads = jnp.zeros(cotangent.shape, jnp.bfloat16)
    grad_state = tuple((jnp.zeros(member.shape, jnp.float32) for member in weights))
    small_sums = tuple((jnp.zeros(member.shape, jnp.float32) for member in small))
    for tick_index in range(MICRO + 1):
        micro_step = tick_index - (1 - section_index)
        usable = (micro_step >= 0) & (micro_step < MICRO)
        position = jnp.clip(micro_step, 0, MICRO - 1)
        flag = usable.astype(jnp.float32)
        out_grad = jnp.where(
            section_index == 1,
            out_grads[min(tick_index, MICRO - 1)],
            incoming_grad.astype(jnp.float32),
        )
        segments = segment_ids(lax.dynamic_index_in_dim(lengths, position, 0, keepdims=False), ROWS)
        stored = tuple(
            (lax.dynamic_index_in_dim(stack, position, 0, keepdims=False) for stack in stored_all)
        )
        input_grad, grad_part, small_grads = backward_tick(
            out_grad, stored, segments, slopes, weights, small, grad_state, flag
        )
        grad_state = grad_part
        small_sums = tuple(
            (total + flag * member for total, member in zip(small_sums, small_grads))
        )
        sent_grad = input_grad.astype(jnp.bfloat16)
        in_grads = keep_where(in_grads, position, usable, sent_grad)
        if tick_index < MICRO:
            incoming_grad = shifted(sent_grad, "section", -1)
    head_width = small_sums[2].shape[1]
    hidden_width = small_sums[6].shape[0]
    qkv_full = lax.dynamic_update_slice_in_dim(
        jnp.zeros((3, D), jnp.float32), small_sums[2], tensor_index * head_width, 1
    )
    up_full = lax.dynamic_update_slice_in_dim(
        jnp.zeros((FF,), jnp.float32), small_sums[6], tensor_index * hidden_width, 0
    )
    summed = lax.psum(
        (
            small_sums[0],
            small_sums[1],
            qkv_full,
            small_sums[3],
            small_sums[4],
            small_sums[5],
            up_full,
            small_sums[7],
        ),
        ("dp", "tensor"),
    )
    qkv_bias_grad = lax.dynamic_slice_in_dim(summed[2], tensor_index * head_width, head_width, 1)
    up_bias_grad = lax.dynamic_slice_in_dim(summed[6], tensor_index * hidden_width, hidden_width, 0)
    reduced = (
        lax.psum_scatter(
            grad_state[0].astype(jnp.bfloat16), "dp", scatter_dimension=0, tiled=True
        ).astype(jnp.float32),
        lax.psum_scatter(
            grad_state[1].astype(jnp.bfloat16), "dp", scatter_dimension=0, tiled=True
        ).astype(jnp.float32),
        lax.psum_scatter(
            grad_state[2].astype(jnp.bfloat16), "dp", scatter_dimension=0, tiled=True
        ).astype(jnp.float32),
        lax.psum_scatter(
            grad_state[3].astype(jnp.bfloat16), "dp", scatter_dimension=0, tiled=True
        ).astype(jnp.float32),
    )
    return (
        outputs[None],
        in_grads[None],
        summed[0][None],
        summed[1][None],
        reduced[0][None],
        qkv_bias_grad[None],
        reduced[1][None],
        summed[3][None],
        summed[4][None],
        summed[5][None],
        reduced[2][None],
        up_bias_grad[None],
        reduced[3][None],
        summed[7][None],
    )


def solution(mesh):
    in_specs = (
        P("dp", "tensor", None),
        P("dp", None),
        P("dp", "tensor", None),
        P("section", None),
        P("section", None),
        P("section", "dp", None, "tensor"),
        P("section", None, "tensor"),
        P("section", "dp", "tensor"),
        P("section", None),
        P("section", None),
        P("section", None),
        P("section", "dp", "tensor"),
        P("section", "tensor"),
        P("section", "dp", "tensor"),
        P("section", None),
    )
    out_specs = (
        P("section", "dp", "tensor", None),
        P("section", "dp", "tensor", None),
        P("section", None),
        P("section", None),
        P("section", "dp", None, "tensor"),
        P("section", None, "tensor"),
        P("section", "dp", "tensor"),
        P("section", None),
        P("section", None),
        P("section", None),
        P("section", "dp", "tensor"),
        P("section", "tensor"),
        P("section", "dp", "tensor"),
        P("section", None),
    )
    return jax.shard_map(local, mesh=mesh, in_specs=in_specs, out_specs=out_specs, check_vma=False)
```

profile of v0, /device:TPU:0, one launch (start us, length us, event | category | flops | bytes accessed | tf_op | source)
XLA Modules:
  0.0 941.2 jit_solution(4496016616352723446)
XLA Ops:
  13.5 5.7 all_gather.48
  22.4 35.7 %all-gather.9.cloned.1.call-done = bf16[1,1024,3,512]{3,1,2,0:T(8,128)(2,1)} async-done(((bf16[1,32,3,512]{3,1,2,0:T(8,128)(2,1)}), bf16[1,1024,3,512]{3,1,2,0:T(8,128)(2,1)}) %all-gather.9.cloned.1.call-update) | async-done | bytes 3145744 | tf_op jit(solution)/shard_map/all_gather | solution.py:264
  58.0 3.2 copy.112
  62.2 2.1 bitcast_dynamic-update-slice_fusion.5
  68.3 34.2 %all-gather.11.cloned.1.call-done = bf16[1,1024,512]{2,1,0:T(8,128)(2,1)} async-done(((bf16[1,32,512]{2,1,0:T(8,128)(2,1)}), bf16[1,1024,512]{2,1,0:T(8,128)(2,1)}) %all-gather.11.cloned.1.call-update) | async-done | bytes 1048592 | tf_op jit(solution)/shard_map/all_gather | solution.py:265
  102.5 2.5 convolution_convert_fusion.5
  124.3 6.5 all_gather.51
  130.8 37.8 %all-gather.13.cloned.1.call-done = bf16[1,1024,2048]{2,1,0:T(8,128)(2,1)} async-done(((bf16[1,32,2048]{2,1,0:T(8,128)(2,1)}), bf16[1,1024,2048]{2,1,0:T(8,128)(2,1)}) %all-gather.13.cloned.1.call-update) | async-done | bytes 4194320 | tf_op jit(solution)/shard_map/all_gather | solution.py:266
  170.3 4.3 bitcast_dynamic-update-slice_fusion.2
  174.5 42.1 %all-gather.15.cloned.1.call-done = bf16[1,1024,2048]{2,1,0:T(8,128)(2,1)} async-done(((bf16[1,32,2048]{2,1,0:T(8,128)(2,1)}), bf16[1,1024,2048]{2,1,0:T(8,128)(2,1)}) %all-gather.15.cloned.1.call-update) | async-done | bytes 4194320 | tf_op jit(solution)/shard_map/all_gather | solution.py:267
  216.7 4.7 fusion.78
  223.8 11.2 %reduce-scatter.19.cloned.1.call-done = bf16[64,1024]{1,0:T(8,128)(2,1)} async-done(((bf16[128,1024]{1,0:T(8,128)(2,1)}), bf16[64,1024]{1,0:T(8,128)(2,1)}) %reduce-scatter.19.cloned.1.call-update) | async-done | bytes 131088 | tf_op jit(solution)/shard_map/reduce_scatter | solution.py:153
  237.4 5.2 collective-permute-start
  242.6 5.9 all_gather.58
  253.3 5.6 all_gather.54
  259.6 3.1 bitcast_dynamic-update-slice_fusion.4
  267.2 2.5 convolution_convert_fusion.4
  272.8 2.3 constant_dynamic-slice_fusion.24
  275.1 9.0 reduce-scatter.21.cloned.1.call-done
  289.5 6.0 all_gather.55
  296.2 4.3 bitcast_dynamic-update-slice_fusion.1
  300.6 2.2 fusion.81
  305.1 12.9 %reduce-scatter.23.cloned.1.call-done = bf16[64,1024]{1,0:T(8,128)(2,1)} async-done(((bf16[128,1024]{1,0:T(8,128)(2,1)}), bf16[64,1024]{1,0:T(8,128)(2,1)}) %reduce-scatter.23.cloned.1.call-update) | async-done | bytes 131088 | tf_op jit(solution)/shard_map/reduce_scatter | solution.py:153
  319.7 4.6 collective-permute-start.1
  329.9 6.1 all_gather.56
  336.7 3.1 bitcast_dynamic-update-slice_fusion.3
  344.2 2.5 convolution_convert_fusion.3
  349.7 2.3 constant_dynamic-slice_fusion.23
  352.1 2.2 constant_dynamic-slice_fusion.7
  355.2 8.1 reduce-scatter.25.cloned.1.call-done
  366.4 6.0 all_gather.57
  372.5 4.7 bitcast_dynamic-update-slice_fusion
  377.2 3.4 convert_reduce_fusion.2
  381.5 2.2 fusion.69
  386.3 12.7 %reduce-scatter.29.cloned.1.call-done = bf16[64,1024]{1,0:T(8,128)(2,1)} async-done(((bf16[128,1024]{1,0:T(8,128)(2,1)}), bf16[64,1024]{1,0:T(8,128)(2,1)}) %reduce-scatter.29.cloned.1.call-update) | async-done | bytes 131088 | tf_op jit(solution)/shard_map/reduce_scatter | solution.py:181
  404.0 5.9 all_gather.59
  410.6 2.2 convolution_convert_fusion.11
  426.1 9.5 %reduce-scatter.31.cloned.1.call-done = bf16[64,1024]{1,0:T(8,128)(2,1)} async-done(((bf16[128,1024]{1,0:T(8,128)(2,1)}), bf16[64,1024]{1,0:T(8,128)(2,1)}) %reduce-scatter.31.cloned.1.call-update) | async-done | bytes 131088 | tf_op jit(solution)/shard_map/reduce_scatter | solution.py:213
  445.7 4.9 collective-permute-done.2
  451.5 5.6 all_gather.60
  457.2 4.6 convert_reduce_fusion.1
  462.6 2.2 fusion.72
  471.6 6.4 reduce-scatter.33.cloned.1.call-done
  484.0 5.9 all_gather.61
  490.7 2.2 convolution_convert_fusion.10
  508.2 9.0 reduce-scatter.35.cloned.1.call-done
  525.5 5.7 collective-permute-done.3
  532.3 5.6 all_gather.62
  537.9 4.6 convert_reduce_fusion
  543.3 2.2 fusion.75
  546.8 4.7 fusion.84
  551.6 2.8 fusion.247
  554.4 4.4 reduce-scatter.37.cloned.1.call-done
  564.8 5.9 all_gather.63
  571.5 2.2 convolution_convert_fusion.9
  582.6 3.2 add_convert_fusion.3
  589.9 2.0 fusion.224
  591.9 3.8 add_convert_fusion.2
  599.6 3.2 add_convert_fusion.1
  603.8 2.5 fusion.159
  606.3 2.6 fusion.161
  608.9 4.6 add_convert_fusion
  620.3 280.5 %all-reduce = (f32[1,1024]{1,0:T(1,128)}, f32[1,1024]{1,0:T(1,128)}, f32[3,1024]{1,0:T(4,128)S(1)}, f32[1,1024]{1,0:T(1,128)}, f32[1,1024]{1,0:T(1,128)}, /*inde...) all-reduce(f32[1,1024]{1,0:T(1,128)S(1)} %bitcast.792, ...), channel_id=1, replica_groups=mesh['section'=2,'dp'=32,'tensor'=2] {'dp','tensor'}, use_global_device_ids=true, to_apply=%region_72.73 | all-reduce | flops 13312 | bytes 106496 | tf_op jit(solution)/shard_map/psum | solution.py:350
  907.8 24.6 %reduce-scatter.47.cloned.1.call-done = bf16[32,2048]{1,0:T(8,128)(2,1)} async-done(((bf16[1024,2048]{1,0:T(8,128)(2,1)}), bf16[32,2048]{1,0:T(8,128)(2,1)}) %reduce-scatter.47.cloned.1.call-update) | async-done | bytes 131088 | tf_op jit(solution)/shard_map/reduce_scatter | solution.py:375
  (458 shorter events, 194.2 us)
Async XLA Ops:
  7.2 50.9 %all-gather.9.cloned.1.call-start = ((), (), s32[]{:S(2)}) async-start(), calls=%async_computation.32 | async-start | bytes 3244032 | tf_op jit(solution)/shard_map/all_gather | solution.py:264
  7.9 94.6 %all-gather.11.cloned.1.call-start = ((), (), s32[]{:S(2)}) async-start(), calls=%async_computation.33 | async-start | bytes 1081344 | tf_op jit(solution)/shard_map/all_gather | solution.py:265
  8.7 111.9 %reduce-scatter.17.cloned.1.call-start = ((), (), s32[]{:S(2)}) async-start(), calls=%async_computation.16 | async-start | bytes 393216 | tf_op jit(solution)/shard_map/reduce_scatter | solution.py:142
  12.9 9.5 %copy-start.5 = (f32[2,64,1024]{2,1,0:T(8,128)}, f32[2,64,1024]{2,1,0:T(8,128)S(1)}, u32[]{:S(2)}) copy-start(f32[2,64,1024]{2,1,0:T(8,128)S(1)} %convert_element_type.402) | copy-start | bytes 1572868
  13.1 9.2 copy-start.3
  19.2 45.1 %copy-start.23 = (bf16[128,1024]{1,0:T(8,128)(2,1)}, bf16[128,1024]{1,0:T(8,128)(2,1)S(1)}, u32[]{:S(2)}) copy-start(bf16[128,1024]{1,0:T(8,128)(2,1)S(1)} %all_gather.48) | copy-start | bytes 786436
  66.6 43.9 %copy-start.69 = (f32[8,128]{1,0:T(8,128)}, f32[8,128]{1,0:T(8,128)S(1)}, u32[]{:S(2)}) copy-start(f32[8,128]{1,0:T(8,128)S(1)} %get-tuple-element.289) | copy-start | bytes 12292
  105.0 63.6 %all-gather.13.cloned.1.call-start = ((), (), s32[]{:S(2)}) async-start(), calls=%async_computation.34 | async-start | bytes 4325376 | tf_op jit(solution)/shard_map/all_gather | solution.py:266
  105.6 111.1 %all-gather.15.cloned.1.call-start = ((), (), s32[]{:S(2)}) async-start(), calls=%async_computation.35 | async-start | bytes 4325376 | tf_op jit(solution)/shard_map/all_gather | solution.py:267
  106.2 128.9 %reduce-scatter.19.cloned.1.call-start = ((), (), s32[]{:S(2)}) async-start(), calls=%async_computation.17 | async-start | bytes 393216 | tf_op jit(solution)/shard_map/reduce_scatter | solution.py:153
  111.2 12.3 %copy-start.62 = (f32[1,1024]{1,0:T(1,128)}, f32[1,1024]{1,0:T(1,128)S(1)}, u32[]{:S(2)}) copy-start(f32[1,1024]{1,0:T(1,128)S(1)} %add.798) | copy-start | bytes 12292
  174.5 47.0 %copy-start.92 = (s32[4,1]{0,1:T(1,128)S(1)}, s32[4,1]{0,1:T(1,128)}, u32[]{:S(2)}) copy-start(s32[4,1]{0,1:T(1,128)} %reduce-window.51) | copy-start | bytes 52
  174.5 47.0 %copy-start.93 = (s32[4,1]{0,1:T(1,128)S(1)}, s32[4,1]{0,1:T(1,128)}, u32[]{:S(2)}) copy-start(s32[4,1]{0,1:T(1,128)} %reduce-window.50) | copy-start | bytes 52
  174.5 47.6 %copy-start.90 = (s32[128]{0:T(128)S(1)}, s32[128]{0:T(128)}, u32[]{:S(2)}) copy-start(s32[128]{0:T(128)} %get-tuple-element.325) | copy-start | bytes 1540
  221.4 62.6 %reduce-scatter.21.cloned.1.call-start = ((), (), s32[]{:S(2)}) async-start(), calls=%async_computation.18 | async-start | bytes 393216 | tf_op jit(solution)/shard_map/reduce_scatter | solution.py:142
  237.4 12.9 %collective-permute-start = (bf16[64,1024]{1,0:T(8,128)(2,1)}, bf16[64,1024]{1,0:T(8,128)(2,1)}, u32[]{:S(2)}, u32[]{:S(2)}) collective-permute-start(bf16[64,1024]{1,0:T(8,128)(2,1)} %get-tuple-element.260), channel_id=1, source_target_pairs={{0,64},{1,65},{2,66},{3,67},{4,68},{5,69},{6,70},{7,71},{8,72},{9,... | collective-permute-start | bytes 393224 | tf_op jit(solution)/shard_map/ppermute | solution.py:20
  267.2 33.3 %copy-start.52 = (bf16[8,64,128]{2,1,0:T(8,128)(2,1)}, bf16[8,64,128]{2,1,0:T(8,128)(2,1)S(1)}, u32[]{:S(2)}) copy-start(bf16[8,64,128]{2,1,0:T(8,128)(2,1)S(1)} %convolution_convert_fusion.7) | copy-start | bytes 393220
  269.7 48.4 %reduce-scatter.23.cloned.1.call-start = ((), (), s32[]{:S(2)}) async-start(), calls=%async_computation.19 | async-start | bytes 393216 | tf_op jit(solution)/shard_map/reduce_scatter | solution.py:153
  288.2 12.3 %copy-start.94 = (bf16[1,1024,2048]{2,1,0:T(8,128)(2,1)S(1)}, bf16[1,1024,2048]{2,1,0:T(8,128)(2,1)}, u32[]{:S(2)}) copy-start(bf16[1,1024,2048]{2,1,0:T(8,128)(2,1)} %all-gather.15.cloned.1.call-done) | copy-start | bytes 12582916
  300.5 17.5 %copy-start.8 = (f32[64,1024]{1,0:T(8,128)S(1)}, f32[64,1024]{1,0:T(8,128)}, u32[]{:S(2)}) copy-start(f32[64,1024]{1,0:T(8,128)} %get-tuple-element.254) | copy-start | bytes 786436
  302.8 60.5 %reduce-scatter.25.cloned.1.call-start = ((), (), s32[]{:S(2)}) async-start(), calls=%async_computation.20 | async-start | bytes 393216 | tf_op jit(solution)/shard_map/reduce_scatter | solution.py:142
  319.7 7.3 collective-permute-start.1
  328.7 15.5 %copy-start.7 = (f32[64,1024]{1,0:T(8,128)}, f32[64,1024]{1,0:T(8,128)S(1)}, u32[]{:S(2)}) copy-start(f32[64,1024]{1,0:T(8,128)S(1)} %get-tuple-element.248) | copy-start | bytes 786436
  344.2 7.8 copy-start.53
  346.7 25.8 %copy-start.57 = (f32[1,2048]{1,0:T(1,128)S(1)}, f32[1,2048]{1,0:T(1,128)}, u32[]{:S(2)}) copy-start(f32[1,2048]{1,0:T(1,128)} %add.803) | copy-start | bytes 24580
  346.7 52.3 %reduce-scatter.29.cloned.1.call-start = ((), (), s32[]{:S(2)}) async-start(), calls=%async_computation.22 | async-start | bytes 393216 | tf_op jit(solution)/shard_map/reduce_scatter | solution.py:181
  365.5 11.7 %copy-start.46 = (bf16[128,1024]{1,0:T(8,128)(2,1)S(1)}, bf16[128,1024]{1,0:T(8,128)(2,1)}, u32[]{:S(2)}) copy-start(bf16[128,1024]{1,0:T(8,128)(2,1)} %all_gather.58) | copy-start | bytes 786436
  365.5 11.7 %copy-start.95 = (bf16[1,1024,2048]{2,1,0:T(8,128)(2,1)S(1)}, bf16[1,1024,2048]{2,1,0:T(8,128)(2,1)}, u32[]{:S(2)}) copy-start(bf16[1,1024,2048]{2,1,0:T(8,128)(2,1)} %all-gather.15.cloned.1.call-done) | copy-start | bytes 12582916
  372.5 8.2 copy-start.24
  377.2 4.3 copy-start
  383.7 51.8 %reduce-scatter.31.cloned.1.call-start = ((), (), s32[]{:S(2)}) async-start(), calls=%async_computation.23 | async-start | bytes 393216 | tf_op jit(solution)/shard_map/reduce_scatter | solution.py:213
  420.3 57.8 %reduce-scatter.33.cloned.1.call-start = ((), (), s32[]{:S(2)}) async-start(), calls=%async_computation.24 | async-start | bytes 393216 | tf_op jit(solution)/shard_map/reduce_scatter | solution.py:181
  441.7 8.8 collective-permute-start.2
  445.6 5.9 copy-start.15
  457.2 4.6 copy-start.48
  457.2 5.4 copy-start.1
  464.8 52.3 %reduce-scatter.35.cloned.1.call-start = ((), (), s32[]{:S(2)}) async-start(), calls=%async_computation.25 | async-start | bytes 393216 | tf_op jit(solution)/shard_map/reduce_scatter | solution.py:213
  501.9 56.9 %reduce-scatter.37.cloned.1.call-start = ((), (), s32[]{:S(2)}) async-start(), calls=%async_computation.26 | async-start | bytes 393216 | tf_op jit(solution)/shard_map/reduce_scatter | solution.py:181
  522.6 8.6 collective-permute-start.3
  537.9 4.6 copy-start.50
  537.9 5.4 copy-start.2
  545.6 69.4 %reduce-scatter.27.cloned.1.call-start = ((), (), s32[]{:S(2)}) async-start(), calls=%async_computation.21 | async-start | bytes 393216 | tf_op jit(solution)/shard_map/reduce_scatter | solution.py:153
  551.5 66.3 %reduce-scatter.39.cloned.1.call-start = ((), (), s32[]{:S(2)}) async-start(), calls=%async_computation.27 | async-start | bytes 393216 | tf_op jit(solution)/shard_map/reduce_scatter | solution.py:213
  581.1 5.1 copy-start.22
  581.1 322.1 %reduce-scatter.43.cloned.1.call-start = ((), (), s32[]{:S(2)}) async-start(), calls=%async_computation.29 | async-start | bytes 1081344 | tf_op jit(solution)/shard_map/reduce_scatter | solution.py:369
  582.6 5.3 copy-start.40
  585.9 318.7 %reduce-scatter.41.cloned.1.call-start = ((), (), s32[]{:S(2)}) async-start(), calls=%async_computation.28 | async-start | bytes 3244032 | tf_op jit(solution)/shard_map/reduce_scatter | solution.py:366
  595.8 310.4 %reduce-scatter.45.cloned.1.call-start = ((), (), s32[]{:S(2)}) async-start(), calls=%async_computation.30 | async-start | bytes 4325376 | tf_op jit(solution)/shard_map/reduce_scatter | solution.py:372
  602.8 329.6 %reduce-scatter.47.cloned.1.call-start = ((), (), s32[]{:S(2)}) async-start(), calls=%async_computation.31 | async-start | bytes 4325376 | tf_op jit(solution)/shard_map/reduce_scatter | solution.py:375
  613.6 4.2 copy-start.73
  613.6 4.2 copy-start.78
  613.6 4.2 copy-start.85
  613.6 4.2 copy-start.77
  613.6 4.2 copy-start.83
  613.6 4.2 copy-start.81
  613.6 4.2 copy-start.82
  613.7 4.2 copy-start.4
  613.7 6.6 copy-start.74
  613.7 6.6 copy-start.79
  613.7 6.6 copy-start.75
  613.7 6.6 copy-start.80
  613.7 288.3 %copy-start.30 = (f32[64,1024]{1,0:T(8,128)S(1)}, f32[64,1024]{1,0:T(8,128)}, u32[]{:S(2)}) copy-start(f32[64,1024]{1,0:T(8,128)} %copy-done.29) | copy-start | bytes 786436
  616.0 318.1 %copy-start.56 = (bf16[1,2,64,1024]{3,2,1,0:T(8,128)(2,1)}, bf16[1,2,64,1024]{3,2,1,0:T(8,128)(2,1)S(1)}, u32[]{:S(2)}) copy-start(bf16[1,2,64,1024]{3,2,1,0:T(8,128)(2,1)S(1)} %fusion.259) | copy-start | bytes 786436
  903.1 30.9 %copy-start.55 = (bf16[1,2,64,1024]{3,2,1,0:T(8,128)(2,1)}, bf16[1,2,64,1024]{3,2,1,0:T(8,128)(2,1)S(1)}, u32[]{:S(2)}) copy-start(bf16[1,2,64,1024]{3,2,1,0:T(8,128)(2,1)S(1)} %fusion.262) | copy-start | bytes 786436
  (56 other events, 102.6 us)
Sparse Core Ops, SparseCore 0:
  10.3 47.6 all-gather.8
  60.3 42.1 all-gather.10
  105.4 13.3 reduce-scatter.16
  121.2 47.3 all-gather.12
  171.0 45.6 all-gather.14
  221.6 13.4 reduce-scatter.18
  269.8 14.2 reduce-scatter.20
  302.9 15.0 reduce-scatter.22
  346.8 16.4 reduce-scatter.24
  383.9 15.1 reduce-scatter.28
  420.4 15.1 reduce-scatter.30
  465.0 13.0 reduce-scatter.32
  502.0 15.1 reduce-scatter.34
  545.7 13.0 reduce-scatter.36
  561.5 15.1 reduce-scatter.26
  581.2 15.1 reduce-scatter.38
  599.7 78.6 reduce-scatter.42
  682.4 79.8 reduce-scatter.40
  765.9 81.2 reduce-scatter.44
  851.1 81.2 reduce-scatter.46
where the time goes:
time: 953 us; the launch traced here: 941 us
  blocking collectives  351 us (37%)
  waiting for transfers between devices  271 us (28%)
  matrix products  119 us (12%)
  other arithmetic  105 us (11%)
  local copies, waits for them, and re-layouts  64.8 us (7%)
  between operations  16.1 us (2%)
  starting transfers between devices  13.8 us (1%)
    psum x1, blocking collectives, local(): lax.psum((small_sums[0], small_sums[1], qkv_full, small_sums[3], small_su...  280 us
    all_gather x1, waiting for transfers between devices, local(): lax.all_gather(shards[3], 'dp', axis=0, tiled=True)  42.1 us
    all_gather x1, waiting for transfers between devices, local(): lax.all_gather(shards[2], 'dp', axis=0, tiled=True)  37.8 us
    all_gather x1, waiting for transfers between devices, local(): lax.all_gather(shards[0], 'dp', axis=0, tiled=True)  35.7 us
    all_gather x1, waiting for transfers between devices, local(): lax.all_gather(shards[1], 'dp', axis=0, tiled=True)  34.2 us
    dot_general x12, matrix products, contract_rows(): lax.dot_general(left, right, (((0,), (0,)), ((), ())), preferred_element_...  30.8 us
    dot_general x12, matrix products, contract_last(): lax.dot_general(left, right, (((1,), (1,)), ((), ())), preferred_element_...  29.7 us
    dynamic_update_slice x23, other arithmetic, keep_where(): lax.dynamic_update_index_in_dim(stacked, jnp.where(usable, value, current...  28.6 us
  transfers between devices with their start and end apart: 24, of which 16 were waited for; matrix products, arithmetic and copies ran while one was open for 16% of the time, Pallas kernels for 0%

commit v1 on v0

v1 whole, which is shorter than its diff:
```python
import jax
import jax.numpy as jnp
from jax import lax
from jax.experimental import pallas as pl
from jax.experimental.pallas import tpu as pltpu
from jax.sharding import PartitionSpec as P

D = 1024
HEADS = 16
HEAD_DIM = 64
FF = 4096
ROWS = 128
EPSILON = 1e-05
GELU_A = 0.79788456
GELU_B = 0.044715

SEQS = 2
HALF = 64
HEADS_HERE = HEADS // 2
WIDTH = HEADS_HERE * HEAD_DIM
HIDDEN = FF // 2
QKV_AT = 0
DENSE_AT = 3 * WIDTH
UP_AT = DENSE_AT + WIDTH
DOWN_AT = UP_AT + HIDDEN
COLUMNS = DOWN_AT + HIDDEN
TILE = 512

BF = jnp.bfloat16
F32 = jnp.float32
MESH = pl.DeviceIdType.MESH

NN = (((1,), (0,)), ((), ()))
NT = (((1,), (1,)), ((), ()))
TN = (((0,), (0,)), ((), ()))


def mm(left, right, dims=NN):
    return lax.dot_general(left, right, dims, preferred_element_type=F32)


class Links:
    def __init__(self, send_sems, recv_sems):
        self.send_sems = send_sems
        self.recv_sems = recv_sems
        self.names = {}
        self.started = []

    def index(self, name):
        return self.names.setdefault(name, len(self.names))

    def copy(self, name, src, dst, device):
        i = self.index(name)
        return pltpu.make_async_remote_copy(
            src_ref=src,
            dst_ref=dst,
            send_sem=self.send_sems.at[i],
            recv_sem=self.recv_sems.at[i],
            device_id=device,
            device_id_type=MESH,
        )

    def send(self, name, src, dst, device):
        copy = self.copy(name, src, dst, device)
        copy.start()
        self.started.append(copy)

    def arrived(self, name, landing, device):
        self.copy(name, landing, landing, device).wait_recv()

    def drain(self):
        for copy in self.started:
            copy.wait_send()
        self.started = []


def four(value):
    return lax.rem(value + 8, 4)


class Place:
    def __init__(self):
        self.section = lax.axis_index("section")
        self.tensor = lax.axis_index("tensor")
        dp = lax.axis_index("dp")
        self.core = lax.rem(dp, 2)
        self.y = lax.rem(lax.div(dp, 2), 4)
        self.z = lax.div(dp, 8)
        self.d = 1 - 2 * self.core

    def dp(self, z, y, core):
        return {"dp": (z * 4 + y) * 2 + core}

    def along(self, axis, offset):
        if axis == "y":
            return self.dp(self.z, four(self.y + offset), self.core)
        return self.dp(four(self.z + offset), self.y, self.core)

    def sibling(self):
        return self.dp(self.z, self.y, 1 - self.core)

    def peer(self):
        return {"tensor": 1 - self.tensor}

    def other_section(self):
        return {"section": 1 - self.section}


FIRST = ("y", "z")
SECOND = ("z", "y")


def gather_weights(place, links, w):
    z, y, core, d = place.z, place.y, place.core, place.d

    def piece(half, first, second):
        if half == 0:
            return w.at[four(z + second), four(y + first), core, 0]
        return w.at[four(z + first), four(y + second), core, 1]

    def send(name, half, spot, axis, offset):
        ref = piece(half, *spot)
        links.send(("ag", name, half), ref, ref, place.along(axis, offset))

    def arrived(name, half, spot):
        links.arrived(("ag", name, half), piece(half, *spot), place.sibling())

    def second_sends(half, k, first):
        send(("s+", k), half, (first, 0), SECOND[half], d)
        send(("s-", k), half, (first, 0), SECOND[half], -d)

    firsts = (0, -d, d, 2)
    for half in range(2):
        send("f+", half, (0, 0), FIRST[half], d)
        send("f-", half, (0, 0), FIRST[half], -d)
    for half in range(2):
        second_sends(half, 0, 0)
    for half in range(2):
        arrived("f+", half, (-d, 0))
        send("fr", half, (-d, 0), FIRST[half], d)
        second_sends(half, 1, -d)
    for half in range(2):
        arrived("f-", half, (d, 0))
        second_sends(half, 2, d)
    for half in range(2):
        arrived(("s+", 0), half, (0, -d))
        send(("sr", 0), half, (0, -d), SECOND[half], d)
    for half in range(2):
        arrived("fr", half, (2, 0))
        second_sends(half, 3, 2)

    def group(half, second, of_core):
        if half == 0:
            return w.at[four(z + second), :, of_core, 0]
        return w.at[:, four(y + second), of_core, 1]

    def to_sibling(half, j, second):
        ref = group(half, second, core)
        links.send(("ag", "sib", j, half), ref, ref, place.sibling())

    for half in range(2):
        to_sibling(half, 0, 0)
    for k in range(1, 4):
        for half in range(2):
            arrived(("s+", k), half, (firsts[k], -d))
            send(("sr", k), half, (firsts[k], -d), SECOND[half], d)
    for half in range(2):
        to_sibling(half, 1, -d)
    for k in range(4):
        for half in range(2):
            arrived(("s-", k), half, (firsts[k], d))
    for half in range(2):
        to_sibling(half, 2, d)
    for k in range(4):
        for half in range(2):
            arrived(("sr", k), half, (firsts[k], 2))
    for half in range(2):
        to_sibling(half, 3, 2)
    for j, second in enumerate((0, d, -d, 2)):
        for half in range(2):
            links.arrived(
                ("ag", "sib", j, half), group(half, second, 1 - core), place.sibling()
            )


def add_rows(target, parts):
    def one(j, carry):
        for at in range(0, COLUMNS, 2048):
            cols = pl.ds(at, 2048)
            total = parts[0](j, cols).astype(F32)
            for part in parts[1:]:
                total = total + part(j, cols).astype(F32)
            target(j, cols, total)
        return carry

    lax.fori_loop(0, 4, one, 0)


def scatter_grads(place, links, g, sb, r1, r2, r3, q, outs, small, small_in, small_outs):
    z, y, core, d = place.z, place.y, place.core, place.d
    axes = ("z", "y")
    other_axes = ("y", "z")

    def group(half, offset, of_core):
        if half == 0:
            return g.at[four(z + offset), :, of_core, 0]
        return g.at[:, four(y + offset), of_core, 1]

    def own_part(half, offset):
        def load(j, cols):
            if half == 0:
                return g[four(z + offset), j, core, 0, :, cols]
            return g[j, four(y + offset), core, 1, :, cols]

        return load

    def of(ref, *lead):
        return lambda j, cols: ref[(*lead, j, slice(None), cols)]

    def into(ref, *lead):
        def store(j, cols, value):
            ref[(*lead, j, slice(None), cols)] = value.astype(BF)

        return store

    mine = (0, d, -d, 2)
    theirs = (0, -d, d, 2)
    for slot in (3, 2, 1, 0):
        for half in range(2):
            links.send(
                ("rs", "sib", slot, half),
                group(half, theirs[slot], 1 - core),
                sb.at[half, slot],
                place.sibling(),
            )

    partners = (
        place.peer(),
        place.sibling(),
        place.dp(z, y + 1 - 2 * lax.rem(y, 2), core),
        place.dp(z, 3 - y, core),
        place.dp(z + 1 - 2 * lax.rem(z, 2), y, core),
        place.dp(3 - z, y, core),
    )

    def small_start(step):
        rows = pl.ds(0, 8 if step == 0 else 16)
        links.send(
            ("small", step), small.at[step, rows], small_in.at[step, rows], partners[step]
        )

    def small_end(step):
        rows = pl.ds(0, 8 if step == 0 else 16)
        links.arrived(("small", step), small_in.at[step, rows], partners[step])
        if step == 0:
            small[1, 0:8] = small[0, 0:8] + small_in[0, 0:8]
            small[1, 8:16] = small[0, 8:16]
        else:
            small[step + 1] = small[step] + small_in[step]

    def from_sibling(slot, half):
        links.arrived(("rs", "sib", slot, half), sb.at[half, slot], place.sibling())

    small_start(0)
    for half in range(2):
        from_sibling(3, half)
        add_rows(into(sb, half, 3), [of(sb, half, 3), own_part(half, mine[3])])
        links.send(("rs", "r1", half), sb.at[half, 3], r1.at[half], place.along(axes[half], d))
    small_end(0)
    small_start(1)
    for half in range(2):
        from_sibling(2, half)
        add_rows(into(sb, half, 2), [of(sb, half, 2), own_part(half, mine[2])])
        links.send(("rs", "r3", half), sb.at[half, 2], r3.at[half], place.along(axes[half], -d))
    small_end(1)
    small_start(2)
    for half in range(2):
        from_sibling(1, half)
        links.arrived(("rs", "r1", half), r1.at[half], place.sibling())
        add_rows(
            into(sb, half, 1), [of(sb, half, 1), own_part(half, mine[1]), of(r1, half)]
        )
        links.send(("rs", "r2", half), sb.at[half, 1], r2.at[half], place.along(axes[half], d))
    small_end(2)
    small_start(3)
    for half in range(2):
        from_sibling(0, half)
        links.arrived(("rs", "r3", half), r3.at[half], place.sibling())
        add_rows(
            into(sb, half, 0), [of(sb, half, 0), own_part(half, mine[0]), of(r3, half)]
        )
    small_end(3)
    small_start(4)
    spots = (y, z)
    for half in range(2):
        links.arrived(("rs", "r2", half), r2.at[half], place.sibling())
        add_rows(into(sb, half, 0), [of(sb, half, 0), of(r2, half)])
        links.send(
            ("rs", "q0", half),
            sb.at[half, 0, four(spots[half] + 2)],
            q.at[half, 0],
            place.along(other_axes[half], d),
        )
        links.send(
            ("rs", "q2", half),
            sb.at[half, 0, four(spots[half] - d)],
            q.at[half, 2],
            place.along(other_axes[half], -d),
        )
    small_end(4)
    small_start(5)
    for half in range(2):
        links.arrived(("rs", "q0", half), q.at[half, 0], place.sibling())
        spot = four(spots[half] + d)
        for at in range(0, COLUMNS, 2048):
            cols = pl.ds(at, 2048)
            total = q[half, 0, :, cols].astype(F32) + sb[half, 0, spot, :, cols].astype(F32)
            q[half, 0, :, cols] = total.astype(BF)
        links.send(
            ("rs", "q1", half), q.at[half, 0], q.at[half, 1], place.along(other_axes[half], d)
        )
    small_end(5)
    ends = ((outs[0], QKV_AT), (outs[1], DENSE_AT), (outs[2], UP_AT), (outs[3], DOWN_AT))
    for half in range(2):
        links.arrived(("rs", "q2", half), q.at[half, 2], place.sibling())
        links.arrived(("rs", "q1", half), q.at[half, 1], place.sibling())
        for out, start in ends:
            for at in range(0, out.shape[1], TILE):
                cols = pl.ds(start + at, TILE)
                out[half * 16 : half * 16 + 16, at : at + TILE] = (
                    sb[half, 0, spots[half], :, cols].astype(F32)
                    + q[half, 1, :, cols].astype(F32)
                    + q[half, 2, :, cols].astype(F32)
                )
    n1g, n1s, qkvb, denseb, n2g, n2s, upb, downb = small_outs
    for row, out in enumerate((n1g, n1s, denseb, n2g, n2s, downb)):
        out[...] = small[6, row : row + 1]
    upb[:, 0:D] = small[6, 8:9]
    upb[:, D : 2 * D] = small[6, 9:10]
    qkvb[0, 0:1] = small[6, 10:11, 0:WIDTH]
    qkvb[0, 1:2] = small[6, 10:11, WIDTH : 2 * WIDTH]
    qkvb[0, 2:3] = small[6, 11:12, 0:WIDTH]


def normalise(values):
    mean = jnp.mean(values, axis=-1, keepdims=True)
    centred = values - mean
    inverse = lax.rsqrt(jnp.mean(centred * centred, axis=-1, keepdims=True) + EPSILON)
    return centred * inverse, inverse


def normalise_back(grad, normed, inverse, gain):
    scaled = grad * gain
    one = jnp.mean(scaled, axis=-1, keepdims=True)
    two = jnp.mean(scaled * normed, axis=-1, keepdims=True)
    return inverse * (scaled - one - normed * two)


def column_sum(values):
    return jnp.sum(values, axis=0, keepdims=True)


def both(ref, t, cols=slice(None)):
    return jnp.concatenate([ref[0, t, :, cols], ref[1, t, :, cols]], axis=0)


def put_both(ref, t, cols, value):
    ref[0, t, :, cols] = value[:HALF]
    ref[1, t, :, cols] = value[HALF:]


def whole_columns(w, cols):
    return w[:, :, :, :, :, cols].reshape(D, -1)


def weight_grad(g, left, right, start, count):
    def one(i, carry):
        at = pl.multiple_of(i * 256, 256)
        piece = left[:, :, :, pl.ds(at, 256)].reshape(SEQS * ROWS, 256)
        for col in range(0, count, TILE):
            size = min(TILE, count - col)
            part = right[:, :, :, col : col + size].reshape(SEQS * ROWS, size)
            value = mm(piece, part, TN).astype(BF)
            g[i, :, :, :, :, start + col : start + col + size] = value.reshape(4, 2, 2, 16, size)
        return carry

    lax.fori_loop(0, 4, one, 0)


def add_partial(w, start, count, load, store):
    rows = load()

    def one(i, carry):
        at = pl.multiple_of(i * 256, 256)
        piece = w[i, :, :, :, :, start : start + count].reshape(256, count)
        store(pl.ds(at, 256), mm(rows, piece, NT))
        return carry

    lax.fori_loop(0, 4, one, 0)


def score_bias(lengths, seq):
    queries = lax.broadcasted_iota(jnp.int32, (ROWS, ROWS), 0)
    keys = lax.broadcasted_iota(jnp.int32, (ROWS, ROWS), 1)
    query_segment = jnp.zeros((ROWS, ROWS), jnp.int32)
    key_segment = jnp.zeros((ROWS, ROWS), jnp.int32)
    end = 0
    for doc in range(4):
        end = end + lengths[seq, doc]
        query_segment = query_segment + (queries >= end).astype(jnp.int32)
        key_segment = key_segment + (keys >= end).astype(jnp.int32)
    allowed = (query_segment == key_segment) & (keys <= queries)
    return jnp.where(allowed, 0.0, -1e30), (queries - keys).astype(F32)


def halves_of_pair():
    lanes = lax.broadcasted_iota(jnp.int32, (1, 128), 1).astype(F32)
    low = jnp.where(lanes < HEAD_DIM, 1.0, 0.0).astype(BF)
    high = jnp.where(lanes < HEAD_DIM, 0.0, 1.0).astype(BF)
    return low, high


def main_kernel(
    x_ref, lengths, cot_ref, n1g, n1s, wqkv, qkvb, wdense, denseb, n2g, n2s, wup, upb, wdown, downb,
    y_out, gx_out, dn1g, dn1s, dqkv, dqkvb, ddense, ddenseb, dn2g, dn2s, dup, dupb, ddown, ddownb,
    w, g, sb, r1, r2, r3, q, small, small_in,
    xs, inbox, outbox, a_all, qkv, o_all, p_all, hidden, xh1, xh2, inv1, inv2, c_all, act, slope_u,
    gz_all, gu, gat_all, go, gqkv, part_out, part_in, wide, ghid, send_sems, recv_sems,
):
    place = Place()
    links = Links(send_sems, recv_sems)
    t, other = place.tensor, 1 - place.tensor

    barrier = pltpu.get_barrier_semaphore()
    neighbours = [
        place.along("y", 1),
        place.along("y", -1),
        place.along("z", 1),
        place.along("z", -1),
        place.sibling(),
        place.peer(),
        place.other_section(),
    ]
    for neighbour in neighbours:
        pl.semaphore_signal(barrier, inc=1, device_id=neighbour, device_id_type=MESH)
    for half in range(2):
        rows = slice(half * 16, half * 16 + 16)
        for ref, start in ((wqkv, QKV_AT), (wdense, DENSE_AT), (wup, UP_AT), (wdown, DOWN_AT)):
            w[place.z, place.y, place.core, half, :, start : start + ref.shape[1]] = ref[rows, :]
    pl.semaphore_wait(barrier, len(neighbours))

    gather_weights(place, links, w)

    @pl.when(place.section == 0)
    def _():
        xs[...] = x_ref[...]

    @pl.when(place.section == 1)
    def _():
        links.arrived("forward", inbox, place.other_section())
        xs[...] = inbox[...]

    def share(name, ref):
        links.send(name, ref.at[:, t], ref.at[:, t], place.peer())

    def shared(name, ref):
        links.arrived(name, ref.at[:, other], place.peer())

    gain1, shift1 = n1g[...].astype(F32), n1s[...].astype(F32)
    gain2, shift2 = n2g[...].astype(F32), n2s[...].astype(F32)

    for s in range(SEQS):
        normed, inverse = normalise(xs[s].astype(F32))
        xh1[s] = normed
        inv1[s] = jnp.broadcast_to(inverse, (HALF, 128))
        a_all[s, t] = (normed * gain1 + shift1).astype(BF)
    share("a", a_all)

    def project(half):
        rows = both(a_all, half)
        for kind in range(3):
            cols = slice(kind * WIDTH, (kind + 1) * WIDTH)
            value = mm(rows, whole_columns(w, cols)) + qkvb[0, kind : kind + 1].astype(F32)
            put_both(qkv, half, cols, value.astype(BF))

    project(t)
    shared("a", a_all)
    project(other)

    masks = halves_of_pair()
    tensor_scale = jnp.where(t == 0, 1.0, 2.0 ** (-8.0 * HEADS_HERE / HEADS))

    def attend(s, carry):
        bias, distance = score_bias(lengths, s)
        distance = distance * tensor_scale
        for pair in range(HEADS_HERE // 2):
            cols = slice(pair * 128, pair * 128 + 128)
            queries = qkv[s, :, :, cols].reshape(ROWS, 128)
            keys = qkv[s, :, :, WIDTH + pair * 128 : WIDTH + pair * 128 + 128].reshape(ROWS, 128)
            values = qkv[s, :, :, 2 * WIDTH + pair * 128 : 2 * WIDTH + pair * 128 + 128]
            values = values.reshape(ROWS, 128)
            mixed = None
            for side in range(2):
                head = pair * 2 + side
                slope = 2.0 ** (-8.0 * (head + 1) / HEADS)
                scores = mm(queries * masks[side], keys, NT) * HEAD_DIM ** (-0.5)
                scores = scores + (bias - slope * distance)
                exponent = jnp.exp(scores - jnp.max(scores, axis=-1, keepdims=True))
                chances = exponent / jnp.sum(exponent, axis=-1, keepdims=True)
                p_all[s, head] = chances
                term = mm(chances.astype(BF), values * masks[side])
                mixed = term if mixed is None else mixed + term
            o_all[s, :, :, cols] = mixed.astype(BF).reshape(2, HALF, 128)
        return carry

    lax.fori_loop(0, SEQS, attend, 0)

    def reduce_start(name, k, start, count, source):
        def to_peer(cols, value):
            part_out[k, 0, :, cols] = value[:HALF].astype(BF)
            part_out[k, 1, :, cols] = value[HALF:].astype(BF)

        add_partial(w, start, count, lambda: both(source, other), to_peer)
        links.send(name, part_out.at[k], part_in.at[k], place.peer())

        def keep(cols, value):
            wide[0, :, cols] = value[:HALF]
            wide[1, :, cols] = value[HALF:]

        add_partial(w, start, count, lambda: both(source, t), keep)

    def reduce_end(name, k):
        links.arrived(name, part_in.at[k], place.peer())

    reduce_start("attended", 0, DENSE_AT, WIDTH, o_all)
    reduce_end("attended", 0)
    for s in range(SEQS):
        value = xs[s].astype(F32) + denseb[...].astype(F32)
        value = value + (wide[s] + part_in[0, s].astype(F32))
        hidden[s] = value
        normed, inverse = normalise(value)
        xh2[s] = normed
        inv2[s] = jnp.broadcast_to(inverse, (HALF, 128))
        c_all[s, t] = (normed * gain2 + shift2).astype(BF)
    share("c", c_all)

    def raise_rows(half):
        rows = both(c_all, half)

        def one(i, carry):
            at = pl.multiple_of(i * TILE, TILE)
            u = mm(rows, whole_columns(w, pl.ds(UP_AT + at, TILE)))
            u = u + upb[:, pl.ds(at, TILE)].astype(F32)
            square = u * u
            tanh = jnp.tanh(GELU_A * u * (1.0 + GELU_B * square))
            inner = GELU_A * (1.0 + (3.0 * GELU_B) * square)
            put_both(act, half, pl.ds(at, TILE), (0.5 * u * (1.0 + tanh)).astype(BF))
            slope = 0.5 * (1.0 + tanh) + 0.5 * u * (1.0 - tanh * tanh) * inner
            put_both(slope_u, half, pl.ds(at, TILE), slope)
            return carry

        lax.fori_loop(0, HIDDEN // TILE, one, 0)

    raise_rows(t)
    shared("c", c_all)
    raise_rows(other)
    reduce_start("lowered", 1, DOWN_AT, HIDDEN, act)
    reduce_end("lowered", 1)
    for s in range(SEQS):
        value = hidden[s] + downb[...].astype(F32) + (wide[s] + part_in[1, s].astype(F32))
        outbox[0, s] = value.astype(BF)
        y_out[s] = value.astype(BF)

    @pl.when(place.section == 0)
    def _():
        links.copy("forward", outbox.at[0], inbox, place.other_section()).start()

    @pl.when(place.section == 0)
    def _():
        links.arrived("backward", inbox, place.other_section())
        xs[...] = inbox[...]

    @pl.when(place.section == 1)
    def _():
        xs[...] = cot_ref[...]

    for s in range(SEQS):
        gz_all[s, t] = xs[s]
    share("gz", gz_all)

    def lower_back(half):
        rows = both(gz_all, half)

        def one(i, carry):
            at = pl.multiple_of(i * TILE, TILE)
            value = mm(rows, whole_columns(w, pl.ds(DOWN_AT + at, TILE)))
            value = value * both(slope_u, half, pl.ds(at, TILE))
            put_both(gu, half, pl.ds(at, TILE), value.astype(BF))
            return carry

        lax.fori_loop(0, HIDDEN // TILE, one, 0)

    lower_back(t)
    shared("gz", gz_all)
    lower_back(other)
    reduce_start("gc", 2, UP_AT, HIDDEN, gu)
    weight_grad(g, gz_all, act, DOWN_AT, HIDDEN)
    reduce_end("gc", 2)
    sums = [0.0] * 6
    for s in range(SEQS):
        grad = wide[s] + part_in[2, s].astype(F32)
        normed = xh2[s]
        gy = xs[s].astype(F32)
        sums[3] = sums[3] + column_sum(grad * normed)
        sums[4] = sums[4] + column_sum(grad)
        sums[5] = sums[5] + column_sum(gy)
        value = gy + normalise_back(grad, normed, inv2[s][:, 0:1], gain2)
        ghid[s] = value
        sums[2] = sums[2] + column_sum(value)
        gat_all[s, t] = value.astype(BF)
    share("gat", gat_all)

    def dense_back(half):
        value = mm(both(gat_all, half), whole_columns(w, slice(DENSE_AT, DENSE_AT + WIDTH)))
        put_both(go, half, slice(None), value.astype(BF))

    dense_back(t)
    weight_grad(g, c_all, gu, UP_AT, HIDDEN)
    shared("gat", gat_all)
    dense_back(other)

    def attend_back(s, carry):
        for pair in range(HEADS_HERE // 2):
            cols = slice(pair * 128, pair * 128 + 128)
            queries = qkv[s, :, :, cols].reshape(ROWS, 128)
            keys = qkv[s, :, :, WIDTH + pair * 128 : WIDTH + pair * 128 + 128].reshape(ROWS, 128)
            values = qkv[s, :, :, 2 * WIDTH + pair * 128 : 2 * WIDTH + pair * 128 + 128]
            values = values.reshape(ROWS, 128)
            grads = go[s, :, :, cols].reshape(ROWS, 128)
            totals = [None, None, None]
            for side in range(2):
                chances = p_all[s, pair * 2 + side]
                out_grad = grads * masks[side]
                chance_grad = mm(out_grad, values, NT)
                inner = jnp.sum(chances * chance_grad, axis=-1, keepdims=True)
                score_grad = (chances * (chance_grad - inner)).astype(BF)
                terms = (
                    mm(score_grad, keys * masks[side]),
                    mm(score_grad, queries * masks[side], TN),
                    mm(chances.astype(BF), out_grad, TN),
                )
                totals = [b if a is None else a + b for a, b in zip(totals, terms)]
            scale = HEAD_DIM ** (-0.5)
            for kind, value in enumerate((totals[0] * scale, totals[1] * scale, totals[2])):
                at = kind * WIDTH + pair * 128
                gqkv[s, :, :, at : at + 128] = value.astype(BF).reshape(2, HALF, 128)
        return carry

    lax.fori_loop(0, SEQS, attend_back, 0)
    reduce_start("ga", 3, QKV_AT, 3 * WIDTH, gqkv)
    weight_grad(g, gat_all, o_all, DENSE_AT, WIDTH)
    reduce_end("ga", 3)
    for s in range(SEQS):
        grad = wide[s] + part_in[3, s].astype(F32)
        normed = xh1[s]
        sums[0] = sums[0] + column_sum(grad * normed)
        sums[1] = sums[1] + column_sum(grad)
        value = ghid[s] + normalise_back(grad, normed, inv1[s][:, 0:1], gain1)
        outbox[1, s] = value.astype(BF)
        gx_out[s] = value.astype(BF)

    @pl.when(place.section == 1)
    def _():
        links.copy("backward", outbox.at[1], inbox, place.other_section()).start()

    weight_grad(g, a_all, gqkv, QKV_AT, 3 * WIDTH)

    small[0, 6:8] = jnp.zeros((2, D), F32)
    small[0, 12:16] = jnp.zeros((4, D), F32)
    for row in range(6):
        small[0, row : row + 1] = sums[row]
    for i in range(2):
        piece = gu[:, :, :, i * D : (i + 1) * D].reshape(SEQS * ROWS, D).astype(F32)
        small[0, 8 + i : 9 + i] = column_sum(piece)
    piece = gqkv[:, :, :, 0:D].reshape(SEQS * ROWS, D).astype(F32)
    small[0, 10:11] = column_sum(piece)
    piece = gqkv[:, :, :, D : 3 * WIDTH].reshape(SEQS * ROWS, WIDTH).astype(F32)
    small[0, 11:12, 0:WIDTH] = column_sum(piece)
    small[0, 11:12, WIDTH:D] = jnp.zeros((1, D - WIDTH), F32)

    scatter_grads(
        place, links, g, sb, r1, r2, r3, q, (dqkv, ddense, dup, ddown), small, small_in,
        (dn1g, dn1s, dqkvb, ddenseb, dn2g, dn2s, dupb, ddownb),
    )
    links.drain()

    @pl.when(place.section == 0)
    def _():
        links.copy("forward", outbox.at[0], inbox, place.other_section()).wait_send()

    @pl.when(place.section == 1)
    def _():
        links.copy("backward", outbox.at[1], inbox, place.other_section()).wait_send()


def local(
    layer_input,
    lengths,
    cotangent,
    norm1_gain,
    norm1_shift,
    qkv_weight,
    qkv_bias,
    dense_weight,
    dense_bias,
    norm2_gain,
    norm2_shift,
    up_weight,
    up_bias,
    down_weight,
    down_bias,
):
    share = qkv_weight.shape[1]
    vmem = pl.BlockSpec(memory_space=pltpu.VMEM)
    smem = pl.BlockSpec(memory_space=pltpu.SMEM)
    shape = jax.ShapeDtypeStruct
    tokens = (SEQS, HALF, D)
    row = shape((1, D), F32)
    out_shape = (
        shape(tokens, BF),
        shape(tokens, BF),
        row,
        row,
        shape((share, 3 * WIDTH), F32),
        shape((1, 3, WIDTH), F32),
        shape((share, WIDTH), F32),
        row,
        row,
        row,
        shape((share, HIDDEN), F32),
        shape((1, HIDDEN), F32),
        shape((share, HIDDEN), F32),
        row,
    )
    block = (4, 4, 2, 2, 16, COLUMNS)

    def all_tokens(width, dtype):
        return pltpu.VMEM((SEQS, 2, HALF, width), dtype)

    scratch = [
        pltpu.VMEM(block, BF),
        pltpu.VMEM(block, BF),
        pltpu.VMEM((2, 4, 4, 16, COLUMNS), BF),
        pltpu.VMEM((2, 4, 16, COLUMNS), BF),
        pltpu.VMEM((2, 4, 16, COLUMNS), BF),
        pltpu.VMEM((2, 4, 16, COLUMNS), BF),
        pltpu.VMEM((2, 3, 16, COLUMNS), BF),
        pltpu.VMEM((7, 16, D), F32),
        pltpu.VMEM((6, 16, D), F32),
        pltpu.VMEM(tokens, BF),
        pltpu.VMEM(tokens, BF),
        pltpu.VMEM((2,) + tokens, BF),
        all_tokens(D, BF),
        all_tokens(3 * WIDTH, BF),
        all_tokens(WIDTH, BF),
        pltpu.VMEM((SEQS, HEADS_HERE, ROWS, ROWS), F32),
        pltpu.VMEM(tokens, F32),
        pltpu.VMEM(tokens, F32),
        pltpu.VMEM(tokens, F32),
        pltpu.VMEM((SEQS, HALF, 128), F32),
        pltpu.VMEM((SEQS, HALF, 128), F32),
        all_tokens(D, BF),
        all_tokens(HIDDEN, BF),
        all_tokens(HIDDEN, F32),
        all_tokens(D, BF),
        all_tokens(HIDDEN, BF),
        all_tokens(D, BF),
        all_tokens(WIDTH, BF),
        all_tokens(3 * WIDTH, BF),
        pltpu.VMEM((4,) + tokens, BF),
        pltpu.VMEM((4,) + tokens, BF),
        pltpu.VMEM(tokens, F32),
        pltpu.VMEM(tokens, F32),
        pltpu.SemaphoreType.DMA((80,)),
        pltpu.SemaphoreType.DMA((80,)),
    ]
    outs = pl.pallas_call(
        main_kernel,
        out_shape=out_shape,
        in_specs=[vmem, smem] + [vmem] * 13,
        out_specs=[vmem] * 14,
        scratch_shapes=scratch,
        compiler_params=pltpu.CompilerParams(
            collective_id=0, has_side_effects=True, vmem_limit_bytes=63 * 2**20
        ),
    )(
        layer_input,
        lengths,
        cotangent,
        norm1_gain,
        norm1_shift,
        qkv_weight.reshape(share, 3 * WIDTH),
        qkv_bias,
        dense_weight[0],
        dense_bias,
        norm2_gain,
        norm2_shift,
        up_weight[0],
        up_bias,
        down_weight[0],
        down_bias,
    )
    (y, gx, n1g, n1s, dqkv, qkvb, ddense, denseb, n2g, n2s, dup, upb, ddown, downb) = outs
    return (
        y[None],
        gx[None],
        n1g,
        n1s,
        dqkv.reshape(1, share, 3, WIDTH),
        qkvb,
        ddense[None],
        denseb,
        n2g,
        n2s,
        dup[None],
        upb,
        ddown[None],
        downb,
    )


def solution(mesh):
    in_specs = (
        P("dp", "tensor", None),
        P("dp", None),
        P("dp", "tensor", None),
        P("section", None),
        P("section", None),
        P("section", "dp", None, "tensor"),
        P("section", None, "tensor"),
        P("section", "dp", "tensor"),
        P("section", None),
        P("section", None),
        P("section", None),
        P("section", "dp", "tensor"),
        P("section", "tensor"),
        P("section", "dp", "tensor"),
        P("section", None),
    )
    out_specs = (
        P("section", "dp", "tensor", None),
        P("section", "dp", "tensor", None),
        P("section", None),
        P("section", None),
        P("section", "dp", None, "tensor"),
        P("section", None, "tensor"),
        P("section", "dp", "tensor"),
        P("section", None),
        P("section", None),
        P("section", None),
        P("section", "dp", "tensor"),
        P("section", "tensor"),
        P("section", "dp", "tensor"),
        P("section", None),
    )
    return jax.shard_map(local, mesh=mesh, in_specs=in_specs, out_specs=out_specs, check_vma=False)
```

time: 953 us -> 260 us (0.27)
  blocking collectives: 351 us -> 0 us
  waiting for transfers between devices: 271 us -> 0 us
  Pallas kernels: 0 us -> 242 us
  matrix products: 119 us -> 0 us
  other arithmetic: 105 us -> 0 us
  local copies, waits for them, and re-layouts: 64.8 us -> 13.2 us
  between operations: 16.1 us -> 0.69 us
  starting transfers between devices: 13.8 us -> 0 us
    psum x1 -> x0, blocking collectives: 280 us -> none  [local(): lax.psum((small_sums[0], small_sums[1], qkv_full, small_sums[3], small_su...]
    pallas_call x0 -> x1, Pallas kernels: none -> 242 us  [local(): pl.pallas_call(main_kernel, out_shape=out_shape, in_specs=[vmem, smem] +...]
    all_gather x4 -> x0, waiting for transfers between devices: 150 us -> none  [the longest x1 42.1 us: local(): lax.all_gather(shards[3], 'dp', axis=0, tiled=True)]
    dot_general x57 -> x0, matrix products: 119 us -> none  [the longest x12 30.8 us: contract_rows(): lax.dot_general(left, right, (((0,), (0,)), ((), ())), preferred_element_...]
    reduce_scatter x16 -> x0, waiting for transfers between devices: 108 us -> none  [the longest x1 24.6 us: local(): lax.psum_scatter(grad_state[3].astype(jnp.bfloat16), 'dp', scatter_dimens...]
    all_gather x12 -> x0, blocking collectives: 71 us -> none  [the longest x3 18.5 us: forward_tick(): normed_two_all = lax.all_gather(normed_two, 'tensor', axis=0, tiled=True)]
    reduce_sum x38 -> x0, other arithmetic: 34.3 us -> none  [the longest x12 11.2 us: layer_norm(): jnp.mean(centred * centred, axis=-1, keepdims=True) + EPSILON]
    dynamic_update_slice x24 -> x0, other arithmetic: 28.6 us -> none  [the longest x23 28.6 us: keep_where(): lax.dynamic_update_index_in_dim(stacked, jnp.where(usable, value, current...]
  transfers between devices with their start and end apart: 24 -> 0, of which waited for: 16 -> 0; matrix products, arithmetic and copies ran while one was open for 16% -> 0% of each run, Pallas kernels for 0% -> 0%
where the time goes in v1:
time: 260 us; the launch traced here: 256 us
  Pallas kernels  242 us (93%)
  local copies, waits for them, and re-layouts  13.2 us (5%)
    pallas_call x1, Pallas kernels, local(): pl.pallas_call(main_kernel, out_shape=out_shape, in_specs=[vmem, smem] +...  242 us
    unnamed x42, local copies, waits for them, and re-layouts  12.1 us

profile of v1, /device:TPU:0, one launch (start us, length us, event | category | flops | bytes accessed | tf_op | source)
XLA Modules:
  0.0 256.1 jit_solution(12445290405318922613)
XLA Ops:
  0.6 1.0 copy.32
  1.6 0.7 copy.35
  2.3 242.2 %shard_map.254 = (bf16[2,64,1024]{2,1,0:T(8,128)(2,1)}, bf16[2,64,1024]{2,1,0:T(8,128)(2,1)}, f32[1,1024]{1,0:T(1,128)}, f32[1,1024]{1,0:T(1,128)}, f32[32,1536]...) custom-call(bf16[2,64,1024]{2,1,0:T(8,128)(2,1)} %x_ref.1, ...), custom_call_target="tpu_custom_call" | custom-call | tf_op jit(solution)/shard_map/pallas_call | solution.py:787
  244.5 0.0 copy-start.5
  244.5 0.7 copy-done.5
  245.2 0.6 copy.34
  245.8 1.1 reshape.35
  246.9 0.0 copy-start.3
  246.9 0.7 copy.33
  247.6 0.2 copy-done.3
  247.8 0.0 copy-start.2
  247.8 0.7 copy.48
  248.5 0.3 copy-done.2
  248.9 0.0 copy-start.12
  248.9 0.0 copy-start.4
  248.9 0.0 copy-start.1
  248.9 0.7 copy.49
  249.6 0.0 copy-done.12
  249.6 0.0 copy-start.11
  249.6 0.6 copy.50
  250.2 0.1 copy-done.11
  250.3 0.6 copy.51
  250.9 0.0 copy-done.4
  250.9 0.0 copy-start.10
  250.9 0.6 copy.52
  251.5 0.0 copy-done.10
  251.5 0.0 copy-start.9
  251.5 0.6 copy.53
  252.1 0.1 copy-done.9
  252.2 0.0 copy-start.8
  252.2 0.6 copy.54
  252.8 0.1 copy-done.8
  252.9 0.6 copy.55
  253.5 0.0 copy-done.1
  253.5 0.0 copy-start.6
  253.5 0.0 copy-start
  253.5 0.7 copy.56
  254.2 0.0 copy-done.6
  254.2 0.6 copy.57
  254.8 0.0 copy-done
  254.8 0.0 copy-start.7
  254.8 0.7 copy.58
  255.5 0.0 copy-done.7
  255.5 0.6 copy.59
Async XLA Ops:
  244.5 0.7 copy-start.5
  246.9 1.0 copy-start.3
  247.8 1.0 copy-start.2
  248.9 0.7 copy-start.12
  248.9 2.0 copy-start.4
  248.9 4.6 %copy-start.1 = (f32[32,2048]{1,0:T(8,128)S(1)}, f32[32,2048]{1,0:T(8,128)}, u32[]{:S(2)}) copy-start(f32[32,2048]{1,0:T(8,128)} %get-tuple-element.38) | copy-start | bytes 786436
  249.6 0.7 copy-start.11
  250.9 0.7 copy-start.10
  251.5 0.7 copy-start.9
  252.2 0.7 copy-start.8
  253.5 0.7 copy-start.6
  253.5 1.3 copy-start
  254.8 0.7 copy-start.7

commit v2 on v1

v2 whole, which is shorter than its diff:
```python
import jax
import jax.numpy as jnp
from jax import lax
from jax.experimental import pallas as pl
from jax.experimental.pallas import tpu as pltpu
from jax.sharding import PartitionSpec as P

D = 1024
HEADS = 16
HEAD_DIM = 64
FF = 4096
ROWS = 128
EPSILON = 1e-05
GELU_A = 0.79788456
GELU_B = 0.044715

SEQS = 2
HALF = 64
HEADS_HERE = HEADS // 2
WIDTH = HEADS_HERE * HEAD_DIM
HIDDEN = FF // 2
QKV_AT = 0
DENSE_AT = 3 * WIDTH
UP_AT = DENSE_AT + WIDTH
DOWN_AT = UP_AT + HIDDEN
COLUMNS = DOWN_AT + HIDDEN
TILE = 512
GROUP = 2048
GROUP_QD, GROUP_UP, GROUP_DOWN = 0, 1, 2

BF = jnp.bfloat16
F32 = jnp.float32
MESH = pl.DeviceIdType.MESH

NN = (((1,), (0,)), ((), ()))
NT = (((1,), (1,)), ((), ()))
TN = (((0,), (0,)), ((), ()))


def mm(left, right, dims=NN):
    return lax.dot_general(left, right, dims, preferred_element_type=F32)


class Links:
    def __init__(self, send_sems, recv_sems):
        self.send_sems = send_sems
        self.recv_sems = recv_sems
        self.names = {}
        self.sources = {}

    def index(self, name):
        return self.names.setdefault(name, len(self.names))

    def copy(self, name, src, dst, device):
        i = self.index(name)
        return pltpu.make_async_remote_copy(
            src_ref=src,
            dst_ref=dst,
            send_sem=self.send_sems.at[i],
            recv_sem=self.recv_sems.at[i],
            device_id=device,
            device_id_type=MESH,
        )

    def send(self, name, source, dst, device):
        self.copy(name, source(), dst, device).start()
        self.sources.setdefault(name, source)

    def arrived(self, name, landing, device):
        self.copy(name, landing, landing, device).wait_recv()

    def drain(self, device):
        for name, source in self.sources.items():
            ref = source()
            self.copy(name, ref, ref, device).wait_send()
        self.sources = {}


def four(value):
    return lax.rem(value + 8, 4)


class Place:
    def __init__(self):
        self.section = lax.axis_index("section")
        self.tensor = lax.axis_index("tensor")
        dp = lax.axis_index("dp")
        self.core = lax.rem(dp, 2)
        self.y = lax.rem(lax.div(dp, 2), 4)
        self.z = lax.div(dp, 8)
        self.d = 1 - 2 * self.core
        self.back = -self.d

    def dp(self, z, y, core):
        return {"dp": (z * 4 + y) * 2 + core}

    def along(self, axis, offset):
        if axis == "y":
            return self.dp(self.z, four(self.y + offset), self.core)
        return self.dp(four(self.z + offset), self.y, self.core)

    def sibling(self):
        return self.dp(self.z, self.y, 1 - self.core)

    def peer(self):
        return {"tensor": 1 - self.tensor}

    def other_section(self):
        return {"section": 1 - self.section}


FIRST = ("y", "z")
SECOND = ("z", "y")


def gather_steps(place, links, w, number):
    z, y, core, d, back = place.z, place.y, place.core, place.d, place.back
    cols = pl.ds(number * GROUP, GROUP)
    firsts = (0, back, d, 2)
    halves = range(2)

    def piece(half, first, second):
        if half == 0:
            return w.at[four(z + second), four(y + first), core, 0, :, cols]
        return w.at[four(z + first), four(y + second), core, 1, :, cols]

    def name_of(name, half):
        return ("gather", number, name, half)

    def send(name, half, spot, axis, offset):
        links.send(
            name_of(name, half),
            lambda: piece(half, *spot),
            piece(half, *spot),
            place.along(axis, offset),
        )

    def arrived(name, half, spot):
        links.arrived(name_of(name, half), piece(half, *spot), place.sibling())

    def second_sends(half, k):
        send(("s+", k), half, (firsts[k], 0), SECOND[half], d)
        send(("s-", k), half, (firsts[k], 0), SECOND[half], back)

    def relay(half, k):
        arrived(("s+", k), half, (firsts[k], back))
        send(("sr", k), half, (firsts[k], back), SECOND[half], d)

    def group(half, second, of_core):
        if half == 0:
            return w.at[four(z + second), :, of_core, 0, :, cols]
        return w.at[:, four(y + second), of_core, 1, :, cols]

    def to_sibling(j, second):
        for half in halves:
            links.send(
                name_of(("swap", j), half),
                lambda half=half: group(half, second, core),
                group(half, second, core),
                place.sibling(),
            )

    def step0():
        for half in halves:
            send("f+", half, (0, 0), FIRST[half], d)
            send("f-", half, (0, 0), FIRST[half], back)
        for half in halves:
            second_sends(half, 0)

    def step1():
        for half in halves:
            arrived("f+", half, (back, 0))
            send("fr", half, (back, 0), FIRST[half], d)
            second_sends(half, 1)

    def step2():
        for half in halves:
            arrived("f-", half, (d, 0))
            second_sends(half, 2)
        for half in halves:
            relay(half, 0)

    def step3():
        for half in halves:
            arrived("fr", half, (2, 0))
            second_sends(half, 3)
        to_sibling(0, 0)

    def step4():
        for k in (1, 2):
            for half in halves:
                relay(half, k)

    def step5():
        for half in halves:
            relay(half, 3)
        to_sibling(1, back)

    def step6():
        for k in range(4):
            for half in halves:
                arrived(("s-", k), half, (firsts[k], d))
        to_sibling(2, d)

    def step7():
        for k in range(4):
            for half in halves:
                arrived(("sr", k), half, (firsts[k], 2))
        to_sibling(3, 2)

    def step8():
        for j, second in enumerate((0, d, back, 2)):
            for half in halves:
                links.arrived(
                    name_of(("swap", j), half), group(half, second, 1 - core), place.sibling()
                )

    return (step0, step1, step2, step3, step4, step5, step6, step7, step8)


def scatter_steps(place, links, g, number, sb, r1, r2, r3, q, finish):
    z, y, core, d, back = place.z, place.y, place.core, place.d, place.back
    start = number * GROUP
    all_cols = pl.ds(start, GROUP)
    axes, other_axes = ("z", "y"), ("y", "z")
    spots = (y, z)
    mine, theirs = (0, d, back, 2), (0, back, d, 2)
    halves = range(2)

    def name_of(name, half):
        return ("scatter", number, name, half)

    def group(half, offset, of_core):
        if half == 0:
            return g.at[four(z + offset), :, of_core, 0, :, all_cols]
        return g.at[:, four(y + offset), of_core, 1, :, all_cols]

    def own(half, offset, j):
        if half == 0:
            return g[four(z + offset), j, core, 0, :, all_cols].astype(F32)
        return g[j, four(y + offset), core, 1, :, all_cols].astype(F32)

    def add(half, slot, with_own, *others):
        def one(j, carry):
            total = sb[number, half, slot, j].astype(F32)
            if with_own:
                total = total + own(half, mine[slot], j)
            for other in others:
                total = total + other[number, half, j].astype(F32)
            sb[number, half, slot, j] = total.astype(BF)
            return carry

        lax.fori_loop(0, 4, one, 0)

    def swapped(half, slot):
        links.arrived(name_of(("swap", slot), half), sb.at[number, half, slot], place.sibling())

    def landed(name, half, ref):
        links.arrived(name_of(name, half), ref, place.sibling())

    def step0():
        for slot in (3, 2, 1, 0):
            for half in halves:
                links.send(
                    name_of(("swap", slot), half),
                    lambda slot=slot, half=half: group(half, theirs[slot], 1 - core),
                    sb.at[number, half, slot],
                    place.sibling(),
                )

    def first_send(name, half, slot, to, offset):
        links.send(
            name_of(name, half),
            lambda: sb.at[number, half, slot],
            to.at[number, half],
            place.along(axes[half], offset),
        )

    def step1():
        for half in halves:
            swapped(half, 3)
            add(half, 3, True)
            first_send("r1", half, 3, r1, d)

    def step2():
        for half in halves:
            swapped(half, 2)
            add(half, 2, True)
            first_send("r3", half, 2, r3, back)

    def step3():
        for half in halves:
            swapped(half, 1)
            landed("r1", half, r1.at[number, half])
            add(half, 1, True, r1)
            first_send("r2", half, 1, r2, d)

    def step4():
        for half in halves:
            swapped(half, 0)
            landed("r3", half, r3.at[number, half])
            add(half, 0, True, r3)

    def second_send(name, half, src, to, offset):
        links.send(name_of(name, half), src, to, place.along(other_axes[half], offset))

    def step5():
        for half in halves:
            landed("r2", half, r2.at[number, half])
            add(half, 0, False, r2)
            for name, way, slot, offset in (("q0", 2, 0, d), ("q2", back, 2, back)):
                second_send(
                    name,
                    half,
                    lambda half=half, way=way: sb.at[number, half, 0, four(spots[half] + way)],
                    q.at[number, half, slot],
                    offset,
                )

    def step6():
        for half in halves:
            landed("q0", half, q.at[number, half, 0])
            total = q[number, half, 0].astype(F32)
            total = total + sb[number, half, 0, four(spots[half] + d)].astype(F32)
            q[number, half, 0] = total.astype(BF)
            second_send(
                "q1", half, lambda half=half: q.at[number, half, 0], q.at[number, half, 1], d
            )

    def step7():
        for half in halves:
            landed("q2", half, q.at[number, half, 2])
            landed("q1", half, q.at[number, half, 1])

            def value(at):
                cols = pl.ds(at, TILE)
                return (
                    sb[number, half, 0, spots[half], :, cols].astype(F32)
                    + q[number, half, 1, :, cols].astype(F32)
                    + q[number, half, 2, :, cols].astype(F32)
                )

            finish(slice(half * 16, half * 16 + 16), value)

    return (step0, step1, step2, step3, step4, step5, step6, step7)


def small_steps(place, links, small, small_in):
    z, y, core = place.z, place.y, place.core
    partners = (
        place.peer(),
        place.sibling(),
        place.dp(z, y + 1 - 2 * lax.rem(y, 2), core),
        place.dp(z, 3 - y, core),
        place.dp(z + 1 - 2 * lax.rem(z, 2), y, core),
        place.dp(3 - z, y, core),
    )

    def rows_of(step):
        return pl.ds(0, 8 if step == 0 else 16)

    def begin(step):
        rows = rows_of(step)
        links.send(
            ("small", step),
            lambda: small.at[step, rows],
            small_in.at[step, rows],
            partners[step],
        )

    def end(step):
        links.arrived(("small", step), small_in.at[step, rows_of(step)], partners[step])
        if step == 0:
            small[1, 0:8] = small[0, 0:8] + small_in[0, 0:8]
            small[1, 8:16] = small[0, 8:16]
        else:
            small[step + 1] = small[step] + small_in[step]

    def at(step):
        def run():
            if step > 0:
                end(step - 1)
            if step < 6:
                begin(step)

        return run

    return tuple(at(step) for step in range(7))


def normalise(values):
    mean = jnp.mean(values, axis=-1, keepdims=True)
    centred = values - mean
    inverse = lax.rsqrt(jnp.mean(centred * centred, axis=-1, keepdims=True) + EPSILON)
    return centred * inverse, inverse


def normalise_back(grad, normed, inverse, gain):
    scaled = grad * gain
    one = jnp.mean(scaled, axis=-1, keepdims=True)
    two = jnp.mean(scaled * normed, axis=-1, keepdims=True)
    return inverse * (scaled - one - normed * two)


def column_sum(values):
    return jnp.sum(values, axis=0, keepdims=True)


def whole_columns(w, cols):
    return w[:, :, :, :, :, cols].reshape(D, -1)


def weight_grad(g, left, right, start, count):
    def one(i, carry):
        at = pl.multiple_of(i * 256, 256)
        piece = left[:, :, :, pl.ds(at, 256)].reshape(SEQS * ROWS, 256)
        for col in range(0, count, TILE):
            size = min(TILE, count - col)
            part = right[:, :, :, col : col + size].reshape(SEQS * ROWS, size)
            value = mm(piece, part, TN).astype(BF)
            g[i, :, :, :, :, start + col : start + col + size] = value.reshape(4, 2, 2, 16, size)
        return carry

    lax.fori_loop(0, 4, one, 0)


def score_bias(lengths, seq):
    queries = lax.broadcasted_iota(jnp.int32, (ROWS, ROWS), 0)
    keys = lax.broadcasted_iota(jnp.int32, (ROWS, ROWS), 1)
    query_segment = jnp.zeros((ROWS, ROWS), jnp.int32)
    key_segment = jnp.zeros((ROWS, ROWS), jnp.int32)
    end = 0
    for doc in range(4):
        end = end + lengths[seq, doc]
        query_segment = query_segment + (queries >= end).astype(jnp.int32)
        key_segment = key_segment + (keys >= end).astype(jnp.int32)
    allowed = (query_segment == key_segment) & (keys <= queries)
    return jnp.where(allowed, 0.0, -1e30), (queries - keys).astype(F32)


def halves_of_pair():
    lanes = lax.broadcasted_iota(jnp.int32, (1, 128), 1).astype(F32)
    low = jnp.where(lanes < HEAD_DIM, 1.0, 0.0).astype(BF)
    high = jnp.where(lanes < HEAD_DIM, 0.0, 1.0).astype(BF)
    return low, high


def main_kernel(
    x_ref, lengths, cot_ref, n1g, n1s, wqkv, qkvb, wdense, denseb, n2g, n2s, wup, upb, wdown, downb,
    y_out, gx_out, dn1g, dn1s, dqkv, dqkvb, ddense, ddenseb, dn2g, dn2s, dup, dupb, ddown, ddownb,
    w, g, sb, r1, r2, r3, q, small, small_in,
    xs, inbox, outbox, a_all, qkv, o_all, p_all, hidden, xh1, xh2, inv1, inv2, c_all, act, slope_u,
    gz_all, gu, gat_all, go, gqkv, part_out, part_in, wide, ghid, send_sems, recv_sems,
):
    place = Place()
    links = Links(send_sems, recv_sems)
    t, other = place.tensor, 1 - place.tensor
    streams = range(SEQS)

    def at_section(number, *steps):
        @pl.when(place.section == number)
        def _():
            for step in steps:
                step()

    barrier = pltpu.get_barrier_semaphore()
    neighbours = [
        place.along("y", 1),
        place.along("y", -1),
        place.along("z", 1),
        place.along("z", -1),
        place.sibling(),
        place.peer(),
        place.other_section(),
    ]
    for neighbour in neighbours:
        pl.semaphore_signal(barrier, inc=1, device_id=neighbour, device_id_type=MESH)
    for half in range(2):
        rows = slice(half * 16, half * 16 + 16)
        here = w.at[place.z, place.y, place.core, half]
        for kind in range(3):
            here[:, kind * WIDTH : (kind + 1) * WIDTH] = wqkv[0, kind, rows, :]
        for ref, start in ((wdense, DENSE_AT), (wup, UP_AT), (wdown, DOWN_AT)):
            here[:, start : start + ref.shape[2]] = ref[0, rows, :]
    pl.semaphore_wait(barrier, len(neighbours))

    def share(name, ref, s):
        links.send((name, s), lambda: ref.at[s, t], ref.at[s, t], place.peer())

    def shared(name, ref, s):
        links.arrived((name, s), ref.at[s, other], place.peer())

    def partial(name, k, s, start, count, source):
        rows = jnp.concatenate([source[s, other], source[s, t]], axis=0)

        def one(i, carry):
            cols = pl.ds(pl.multiple_of(i * 256, 256), 256)
            value = mm(rows, w[i, :, :, :, :, start : start + count].reshape(256, count), NT)
            part_out[k, s, :, cols] = value[:HALF].astype(BF)
            wide[k % 2, s, :, cols] = value[HALF:]
            return carry

        lax.fori_loop(0, 4, one, 0)
        links.send((name, s), lambda: part_out.at[k, s], part_in.at[k, s], place.peer())

    def summed(name, k, s):
        links.arrived((name, s), part_in.at[k, s], place.peer())
        return wide[k % 2, s] + part_in[k, s].astype(F32)

    gather = [gather_steps(place, links, w, number) for number in range(3)]

    def all_gathers():
        for step in range(9):
            for number in range(3):
                gather[number][step]()

    def cotangent_shared():
        for s in streams:
            gz_all[s, t] = cot_ref[s]
            share("gz", gz_all, s)

    qd, up, down = gather
    at_section(1, all_gathers, cotangent_shared)
    at_section(0, *qd[0:5], up[0], *qd[5:8], up[1], qd[8])

    gain1, shift1 = n1g[...].astype(F32), n1s[...].astype(F32)
    gain2, shift2 = n2g[...].astype(F32), n2s[...].astype(F32)
    masks = halves_of_pair()
    tensor_scale = jnp.where(t == 0, 1.0, 2.0 ** (-8.0 * HEADS_HERE / HEADS))

    def enter(s):
        @pl.when(place.section == 0)
        def _():
            xs[s] = x_ref[s]

        @pl.when(place.section == 1)
        def _():
            links.arrived(("forward", s), inbox.at[s], place.other_section())
            xs[s] = inbox[s]

        normed, inverse = normalise(xs[s].astype(F32))
        xh1[s] = normed
        inv1[s] = jnp.broadcast_to(inverse, (HALF, 128))
        a_all[s, t] = (normed * gain1 + shift1).astype(BF)
        share("a", a_all, s)

    def project(s):
        shared("a", a_all, s)
        rows = a_all[s].reshape(ROWS, D)
        for kind in range(3):
            cols = slice(kind * WIDTH, (kind + 1) * WIDTH)
            value = mm(rows, whole_columns(w, cols)) + qkvb[0, kind : kind + 1].astype(F32)
            qkv[s, :, :, cols] = value.astype(BF).reshape(2, HALF, WIDTH)

    def heads_of(ref, s, kind, pair):
        at = kind * WIDTH + pair * 128
        return ref[s, :, :, at : at + 128].reshape(ROWS, 128)

    def attend(s):
        bias, distance = score_bias(lengths, s)
        distance = distance * tensor_scale
        for pair in range(HEADS_HERE // 2):
            queries, keys, values = (heads_of(qkv, s, kind, pair) for kind in range(3))
            mixed = None
            for side in range(2):
                head = pair * 2 + side
                slope = 2.0 ** (-8.0 * (head + 1) / HEADS)
                scores = mm(queries * masks[side], keys, NT) * HEAD_DIM ** (-0.5)
                scores = scores + (bias - slope * distance)
                exponent = jnp.exp(scores - jnp.max(scores, axis=-1, keepdims=True))
                chances = exponent / jnp.sum(exponent, axis=-1, keepdims=True)
                p_all[s, head] = chances
                term = mm(chances.astype(BF), values * masks[side])
                mixed = term if mixed is None else mixed + term
            cols = slice(pair * 128, pair * 128 + 128)
            o_all[s, :, :, cols] = mixed.astype(BF).reshape(2, HALF, 128)
        partial("attended", 0, s, DENSE_AT, WIDTH, o_all)

    def middle(s):
        value = xs[s].astype(F32) + denseb[...].astype(F32)
        value = value + summed("attended", 0, s)
        hidden[s] = value
        normed, inverse = normalise(value)
        xh2[s] = normed
        inv2[s] = jnp.broadcast_to(inverse, (HALF, 128))
        c_all[s, t] = (normed * gain2 + shift2).astype(BF)
        share("c", c_all, s)

    def expand(s):
        shared("c", c_all, s)
        rows = c_all[s].reshape(ROWS, D)

        def one(i, carry):
            at = pl.multiple_of(i * TILE, TILE)
            u = mm(rows, whole_columns(w, pl.ds(UP_AT + at, TILE)))
            u = u + upb[:, pl.ds(at, TILE)].astype(F32)
            square = u * u
            tanh = jnp.tanh(GELU_A * u * (1.0 + GELU_B * square))
            inner = GELU_A * (1.0 + (3.0 * GELU_B) * square)
            value = (0.5 * u * (1.0 + tanh)).astype(BF)
            act[s, :, :, pl.ds(at, TILE)] = value.reshape(2, HALF, TILE)
            slope = 0.5 * (1.0 + tanh) + 0.5 * u * (1.0 - tanh * tanh) * inner
            slope_u[s, :, :, pl.ds(at, TILE)] = slope.reshape(2, HALF, TILE)
            return carry

        lax.fori_loop(0, HIDDEN // TILE, one, 0)

    def contract(s):
        partial("lowered", 1, s, DOWN_AT, HIDDEN, act)

    def leave(s):
        value = hidden[s] + downb[...].astype(F32) + summed("lowered", 1, s)
        outbox[0, s] = value.astype(BF)
        y_out[0, s] = value.astype(BF)

    def forward_copy(s):
        return links.copy(("forward", s), outbox.at[0, s], inbox.at[s], place.other_section())

    def backward_copy(s):
        return links.copy(("backward", s), outbox.at[1, s], inbox.at[s], place.other_section())

    enter(0)
    enter(1)
    at_section(0, up[2], up[3])
    project(0)
    at_section(0, up[4], up[5], down[0])
    attend(0)
    at_section(0, up[6], up[7], down[1])
    project(1)
    at_section(0, up[8], down[2], down[3])
    attend(1)
    at_section(0, down[4], down[5])
    middle(0)
    middle(1)
    at_section(0, down[6], down[7])
    expand(0)
    at_section(0, down[8])
    contract(0)
    expand(1)
    contract(1)

    @pl.when(place.section == 0)
    def _():
        for s in streams:
            leave(s)
            forward_copy(s).start()

    @pl.when(place.section == 0)
    def _():
        for s in streams:
            links.arrived(("backward", s), inbox.at[s], place.other_section())
            gz_all[s, t] = inbox[s]
            share("gz", gz_all, s)

    sums = [0.0] * 6

    def contract_back(s):
        shared("gz", gz_all, s)
        rows = gz_all[s].reshape(ROWS, D)

        def one(i, carry):
            at = pl.multiple_of(i * TILE, TILE)
            value = mm(rows, whole_columns(w, pl.ds(DOWN_AT + at, TILE)))
            value = value * slope_u[s, :, :, pl.ds(at, TILE)].reshape(ROWS, TILE)
            gu[s, :, :, pl.ds(at, TILE)] = value.astype(BF).reshape(2, HALF, TILE)
            return carry

        lax.fori_loop(0, HIDDEN // TILE, one, 0)
        partial("gc", 2, s, UP_AT, HIDDEN, gu)

    def middle_back(s):
        grad = summed("gc", 2, s)
        normed = xh2[s]
        gy = gz_all[s, t].astype(F32)
        sums[3] = sums[3] + column_sum(grad * normed)
        sums[4] = sums[4] + column_sum(grad)
        sums[5] = sums[5] + column_sum(gy)
        value = gy + normalise_back(grad, normed, inv2[s][:, 0:1], gain2)
        ghid[s] = value
        sums[2] = sums[2] + column_sum(value)
        gat_all[s, t] = value.astype(BF)
        share("gat", gat_all, s)

    def attend_back(s):
        shared("gat", gat_all, s)
        rows = gat_all[s].reshape(ROWS, D)
        value = mm(rows, whole_columns(w, slice(DENSE_AT, DENSE_AT + WIDTH)))
        go[s] = value.astype(BF).reshape(2, HALF, WIDTH)
        for pair in range(HEADS_HERE // 2):
            queries, keys, values = (heads_of(qkv, s, kind, pair) for kind in range(3))
            grads = heads_of(go, s, 0, pair)
            totals = [None, None, None]
            for side in range(2):
                chances = p_all[s, pair * 2 + side]
                out_grad = grads * masks[side]
                chance_grad = mm(out_grad, values, NT)
                inner = jnp.sum(chances * chance_grad, axis=-1, keepdims=True)
                score_grad = (chances * (chance_grad - inner)).astype(BF)
                terms = (
                    mm(score_grad, keys * masks[side]),
                    mm(score_grad, queries * masks[side], TN),
                    mm(chances.astype(BF), out_grad, TN),
                )
                totals = [b if a is None else a + b for a, b in zip(totals, terms)]
            scale = HEAD_DIM ** (-0.5)
            for kind, value in enumerate((totals[0] * scale, totals[1] * scale, totals[2])):
                at = kind * WIDTH + pair * 128
                gqkv[s, :, :, at : at + 128] = value.astype(BF).reshape(2, HALF, 128)
        partial("ga", 4, s, QKV_AT, 3 * WIDTH, gqkv)

    def leave_back(s):
        grad = summed("ga", 4, s)
        normed = xh1[s]
        sums[0] = sums[0] + column_sum(grad * normed)
        sums[1] = sums[1] + column_sum(grad)
        value = ghid[s] + normalise_back(grad, normed, inv1[s][:, 0:1], gain1)
        outbox[1, s] = value.astype(BF)
        gx_out[0, s] = value.astype(BF)

        @pl.when(place.section == 1)
        def _():
            backward_copy(s).start()

    def finish_qd(rows, value):
        for kind in range(3):
            dqkv[0, kind, rows, :] = value(kind * WIDTH)
        ddense[0, rows, :] = value(DENSE_AT)

    def finish_into(out):
        def finish(rows, value):
            for at in range(0, GROUP, TILE):
                out[0, rows, at : at + TILE] = value(at)

        return finish

    finishes = (finish_qd, finish_into(dup), finish_into(ddown))
    sc_qd, sc_up, sc_down = (
        scatter_steps(place, links, g, number, sb, r1, r2, r3, q, finishes[number])
        for number in range(3)
    )

    def grad_down():
        weight_grad(g, gz_all, act, DOWN_AT, HIDDEN)

    def grad_up():
        weight_grad(g, c_all, gu, UP_AT, HIDDEN)

    contract_back(0)
    contract_back(1)
    at_section(1, lambda: leave(0), lambda: leave(1))
    middle_back(0)
    grad_down()
    at_section(0, sc_down[0])
    middle_back(1)
    at_section(0, grad_up, sc_up[0], sc_down[1])
    attend_back(0)
    at_section(0, sc_down[2], sc_up[1], sc_down[3])
    attend_back(1)
    at_section(0, sc_up[2], sc_down[4], sc_up[3], sc_down[5])
    leave_back(0)
    at_section(0, sc_up[4], sc_down[6])
    leave_back(1)
    at_section(0, sc_up[5], sc_down[7])
    at_section(1, grad_up)
    weight_grad(g, a_all, gqkv, QKV_AT, 3 * WIDTH)
    weight_grad(g, gat_all, o_all, DENSE_AT, WIDTH)
    at_section(0, sc_qd[0], sc_up[6], sc_up[7])

    small[0, 6:8] = jnp.zeros((2, D), F32)
    small[0, 12:16] = jnp.zeros((4, D), F32)
    for row in range(6):
        small[0, row : row + 1] = sums[row]
    for i in range(2):
        piece = gu[:, :, :, i * D : (i + 1) * D].reshape(SEQS * ROWS, D).astype(F32)
        small[0, 8 + i : 9 + i] = column_sum(piece)
    piece = gqkv[:, :, :, 0:D].reshape(SEQS * ROWS, D).astype(F32)
    small[0, 10:11] = column_sum(piece)
    piece = gqkv[:, :, :, D : 3 * WIDTH].reshape(SEQS * ROWS, WIDTH).astype(F32)
    small[0, 11:12, 0:WIDTH] = column_sum(piece)
    small[0, 11:12, WIDTH:D] = jnp.zeros((1, D - WIDTH), F32)

    tiny = small_steps(place, links, small, small_in)
    last = []
    for step in range(1, 8):
        last += [tiny[step - 1], sc_qd[step]]
    at_section(0, *last)
    last = [sc_down[0], sc_up[0], sc_qd[0]]
    for step in range(1, 8):
        last += [tiny[step - 1], sc_down[step], sc_up[step], sc_qd[step]]
    at_section(1, *last)

    for row, out in enumerate((dn1g, dn1s, ddenseb, dn2g, dn2s, ddownb)):
        out[...] = small[6, row : row + 1]
    dupb[:, 0:D] = small[6, 8:9]
    dupb[:, D : 2 * D] = small[6, 9:10]
    dqkvb[0] = small[6, 10:11, 0:WIDTH]
    dqkvb[1] = small[6, 10:11, WIDTH : 2 * WIDTH]
    dqkvb[2] = small[6, 11:12, 0:WIDTH]

    links.drain(place.sibling())
    at_section(0, *(forward_copy(s).wait_send for s in streams))
    at_section(1, *(backward_copy(s).wait_send for s in streams))


def publish_kernel(*refs):
    count = len(refs) // 2
    sems = refs[-1]
    copies = [pltpu.make_async_copy(refs[i], refs[count + i], sems.at[i]) for i in range(count)]
    for copy in copies:
        copy.start()
    for copy in copies:
        copy.wait()


def local(
    layer_input,
    lengths,
    cotangent,
    norm1_gain,
    norm1_shift,
    qkv_weight,
    qkv_bias,
    dense_weight,
    dense_bias,
    norm2_gain,
    norm2_shift,
    up_weight,
    up_bias,
    down_weight,
    down_bias,
):
    share = qkv_weight.shape[1]
    vmem = pl.BlockSpec(memory_space=pltpu.VMEM)
    smem = pl.BlockSpec(memory_space=pltpu.SMEM)
    shape = jax.ShapeDtypeStruct
    tokens = (SEQS, HALF, D)
    tokens_out = shape((1,) + tokens, BF)
    row = shape((1, D), F32)
    out_shape = (
        tokens_out,
        tokens_out,
        row,
        row,
        shape((1, 3, share, WIDTH), F32),
        shape((3, 1, WIDTH), F32),
        shape((1, share, WIDTH), F32),
        row,
        row,
        row,
        shape((1, share, HIDDEN), F32),
        shape((1, HIDDEN), F32),
        shape((1, share, HIDDEN), F32),
        row,
    )
    block = (4, 4, 2, 2, 16, COLUMNS)

    def all_tokens(width, dtype):
        return pltpu.VMEM((SEQS, 2, HALF, width), dtype)

    scratch = [
        pltpu.VMEM(block, BF),
        pltpu.VMEM(block, BF),
        pltpu.VMEM((3, 2, 4, 4, 16, GROUP), BF),
        pltpu.VMEM((3, 2, 4, 16, GROUP), BF),
        pltpu.VMEM((3, 2, 4, 16, GROUP), BF),
        pltpu.VMEM((3, 2, 4, 16, GROUP), BF),
        pltpu.VMEM((3, 2, 3, 16, GROUP), BF),
        pltpu.VMEM((7, 16, D), F32),
        pltpu.VMEM((6, 16, D), F32),
        pltpu.VMEM(tokens, BF),
        pltpu.VMEM(tokens, BF),
        pltpu.VMEM((2,) + tokens, BF),
        all_tokens(D, BF),
        all_tokens(3 * WIDTH, BF),
        all_tokens(WIDTH, BF),
        pltpu.VMEM((SEQS, HEADS_HERE, ROWS, ROWS), F32),
        pltpu.VMEM(tokens, F32),
        pltpu.VMEM(tokens, F32),
        pltpu.VMEM(tokens, F32),
        pltpu.VMEM((SEQS, HALF, 128), F32),
        pltpu.VMEM((SEQS, HALF, 128), F32),
        all_tokens(D, BF),
        all_tokens(HIDDEN, BF),
        all_tokens(HIDDEN, F32),
        all_tokens(D, BF),
        all_tokens(HIDDEN, BF),
        all_tokens(D, BF),
        all_tokens(WIDTH, BF),
        all_tokens(3 * WIDTH, BF),
        pltpu.VMEM((5,) + tokens, BF),
        pltpu.VMEM((5,) + tokens, BF),
        pltpu.VMEM((2,) + tokens, F32),
        pltpu.VMEM(tokens, F32),
        pltpu.SemaphoreType.DMA((208,)),
        pltpu.SemaphoreType.DMA((208,)),
    ]
    outs = pl.pallas_call(
        main_kernel,
        out_shape=out_shape,
        in_specs=[vmem, smem] + [vmem] * 13,
        out_specs=[vmem] * 14,
        scratch_shapes=scratch,
        compiler_params=pltpu.CompilerParams(
            collective_id=0, has_side_effects=True, vmem_limit_bytes=63 * 2**20
        ),
    )(
        layer_input,
        lengths,
        cotangent,
        norm1_gain,
        norm1_shift,
        jnp.transpose(qkv_weight, (0, 2, 1, 3)),
        qkv_bias,
        dense_weight,
        dense_bias,
        norm2_gain,
        norm2_shift,
        up_weight,
        up_bias,
        down_weight,
        down_bias,
    )
    outs = pl.pallas_call(
        publish_kernel,
        out_shape=out_shape,
        in_specs=[pl.BlockSpec(memory_space=pl.ANY)] * 14,
        out_specs=[vmem] * 14,
        scratch_shapes=[pltpu.SemaphoreType.DMA((14,))],
        compiler_params=pltpu.CompilerParams(vmem_limit_bytes=62 * 2**20),
    )(*outs)
    outs = list(outs)
    outs[4] = jnp.transpose(outs[4], (0, 2, 1, 3))
    outs[5] = jnp.transpose(outs[5], (1, 0, 2))
    return tuple(outs)


def solution(mesh):
    in_specs = (
        P("dp", "tensor", None),
        P("dp", None),
        P("dp", "tensor", None),
        P("section", None),
        P("section", None),
        P("section", "dp", None, "tensor"),
        P("section", None, "tensor"),
        P("section", "dp", "tensor"),
        P("section", None),
        P("section", None),
        P("section", None),
        P("section", "dp", "tensor"),
        P("section", "tensor"),
        P("section", "dp", "tensor"),
        P("section", None),
    )
    out_specs = (
        P("section", "dp", "tensor", None),
        P("section", "dp", "tensor", None),
        P("section", None),
        P("section", None),
        P("section", "dp", None, "tensor"),
        P("section", None, "tensor"),
        P("section", "dp", "tensor"),
        P("section", None),
        P("section", None),
        P("section", None),
        P("section", "dp", "tensor"),
        P("section", "tensor"),
        P("section", "dp", "tensor"),
        P("section", None),
    )
    return jax.shard_map(local, mesh=mesh, in_specs=in_specs, out_specs=out_specs, check_vma=False)
```

time: 260 us -> 206 us (0.79); the launches traced: 256 us -> 206 us
  Pallas kernels: 242 us -> 205 us
  local copies, waits for them, and re-layouts: 13.2 us -> 0 us
    pallas_call x1, Pallas kernels: 242 us -> 202 us  [local(): pl.pallas_call(main_kernel, out_shape=out_shape, in_specs=[vmem, smem] +...]
    unnamed x42 -> x0, local copies, waits for them, and re-layouts: 12.1 us -> none
where the time goes in v2:
time: 206 us
  Pallas kernels  205 us (100%)
    pallas_call x1, Pallas kernels, local(): pl.pallas_call(main_kernel, out_shape=out_shape, in_specs=[vmem, smem] +...  202 us

profile of v2, /device:TPU:0, one launch (start us, length us, event | category | flops | bytes accessed | tf_op | source)
XLA Modules:
  0.0 205.8 jit_solution(17752348565405746729)
XLA Ops:
  0.7 202.5 %shard_map.254 = (bf16[1,2,64,1024]{3,2,1,0:T(8,128)(2,1)}, bf16[1,2,64,1024]{3,2,1,0:T(8,128)(2,1)}, f32[1,1024]{1,0:T(1,128)}, f32[1,1024]{1,0:T(1,128)}, f32[...) custom-call(bf16[2,64,1024]{2,1,0:T(8,128)(2,1)} %x_ref.1, ...), custom_call_target="tpu_custom_call" | custom-call | tf_op jit(solution)/shard_map/pallas_call | solution.py:897
  203.1 2.5 %shard_map.255 = (bf16[1,2,64,1024]{3,2,1,0:T(8,128)(2,1)}, bf16[1,2,64,1024]{3,2,1,0:T(8,128)(2,1)}, f32[1,1024]{1,0:T(1,128)}, f32[1,1024]{1,0:T(1,128)}, f32[...) custom-call(bf16[1,2,64,1024]{3,2,1,0:T(8,128)(2,1)} %get-tuple-elem, ...), custom_call_target="tpu_custom_call" | custom-call | tf_op jit(solution)/shard_map/pallas_call | solution.py:923
